TPU v7x, 512 devices: a whole 4x4x16 slice. The times are simulated.
512 devices in a mesh: user: 16 (over y, z_hi), item: 16 (over x, z_lo), layer: 2 (over core).
Axes of the slice: x: 4, y: 4, z: 16 (z_hi: 4, z_lo: 4; z = z_hi * 4 + z_lo), core: 2. Of those that a mesh axis runs over, the one named last changes fastest.
Arguments:
- user_factors: bfloat16 [64, 131072], P(None, ('user', 'item')), may hold values from -6 to 6
- item_factors: bfloat16 [64, 16384], P(None, 'item'), may hold values from -0.75 to 0.75
- ratings: bfloat16 [65536, 128, 128], P(('user', 'item', 'layer')), may hold values from -6 to 6
- masks: int32 [65536, 16, 128], P(('user', 'item', 'layer')), may hold values from 0 to 255
- tile_rows: int32 [65536], P(('user', 'item', 'layer')), may hold values from 0 to 3
- tile_cols: int32 [65536], P(('user', 'item', 'layer')), may hold values from 0 to 7
Outputs:
- grad_users: float32 [64, 131072], P(None, ('user', 'item'))
- grad_items: float32 [64, 16384], P(None, 'item')
All inputs are finite; a program needn't handle non-finite values.
Results may differ from a plain program's by a relative error of at most 0.004.
Values may be sent and summed in bfloat16 or wider, within the bound.
No kernel may reach another device: no remote copies, remote signals or barrier semaphores. Data moves between devices by JAX's collectives and lax.ppermute only.
A program may use at most 64 MiB of HBM per device.

v0:
```python
import jax
import jax.numpy as jnp
from jax import lax
from jax.sharding import PartitionSpec as P

LOSS_SCALE = 0.0625
DECAY = 0.1


def shifted(block, axis, distance):
    devices = range(lax.axis_size(axis))
    route = [((i - distance) % len(devices), i) for i in devices]
    return lax.ppermute(block, axis, route)


def unpack(packed):
    tiles_here, word_count, columns = packed.shape
    bit_place = jnp.arange(8, dtype=jnp.int32)
    bit_values = jnp.bitwise_and(
        jnp.right_shift(packed[:, :, None, :], bit_place[None, None, :, None]), 1
    )
    return bit_values.reshape(tiles_here, word_count * 8, columns).astype(jnp.float32)


def shard_terms(user_cube, item_shard, rating, packed, row_index, col_index):
    rank_len, user_blocks, tile_len = user_cube.shape
    item_blocks = item_shard.shape[1] // tile_len
    row_hot = row_index[:, None] == jnp.arange(user_blocks, dtype=jnp.int32)[None, :]
    col_hot = col_index[:, None] == jnp.arange(item_blocks, dtype=jnp.int32)[None, :]
    user_portion = jnp.einsum(
        "rbk,tb->rtk", user_cube, row_hot.astype(jnp.bfloat16), preferred_element_type=jnp.float32
    ).astype(jnp.bfloat16)
    item_cube = item_shard.reshape(rank_len, item_blocks, tile_len)
    item_portion = jnp.einsum(
        "rbk,tb->rtk", item_cube, col_hot.astype(jnp.bfloat16), preferred_element_type=jnp.float32
    ).astype(jnp.bfloat16)
    predicted_scores = jnp.einsum(
        "bjy,bjf->jyf", user_portion, item_portion, preferred_element_type=jnp.float32
    )
    rating_residual = (unpack(packed) * (predicted_scores - rating.astype(jnp.float32))).astype(
        jnp.bfloat16
    )
    user_increment = jnp.einsum(
        "ydw,kyw->kyd", rating_residual, item_portion, preferred_element_type=jnp.float32
    )
    item_increment = jnp.einsum(
        "nwp,enw->enp", rating_residual, user_portion, preferred_element_type=jnp.float32
    )
    highest_precision = lax.Precision.HIGHEST
    user_back = jnp.einsum(
        "rta,tb->rba", user_increment, row_hot.astype(jnp.float32), precision=highest_precision
    )
    item_back = jnp.einsum(
        "rtc,tb->rbc", item_increment, col_hot.astype(jnp.float32), precision=highest_precision
    )
    return (
        user_back.reshape(rank_len, user_blocks * tile_len),
        item_back.reshape(rank_len, item_blocks * tile_len),
    )


def body(user_factors, item_factors, ratings, masks, tile_rows, tile_cols):
    rank_len, shard_len = item_factors.shape
    tile_len = ratings.shape[1]
    user_blocks = user_factors.shape[1] // tile_len
    user_cube = user_factors.reshape(rank_len, user_blocks, tile_len)
    cycle_size = lax.axis_size("item")
    per_shard = ratings.shape[0] // cycle_size
    position = lax.axis_index("item")

    def select(shard_at):
        start_tile = shard_at * per_shard
        return (
            lax.dynamic_slice_in_dim(ratings, start_tile, per_shard, 0),
            lax.dynamic_slice_in_dim(masks, start_tile, per_shard, 0),
            lax.dynamic_slice_in_dim(tile_rows, start_tile, per_shard, 0),
            lax.dynamic_slice_in_dim(tile_cols, start_tile, per_shard, 0),
        )

    user_start = jnp.zeros((rank_len, user_blocks * tile_len), jnp.float32)

    def cycle_step(offset, state):
        moving, carried, user_grad = state
        shard_at = (position - offset) % cycle_size
        rating, packed, row_index, col_index = select(shard_at)
        user_increment, item_increment = shard_terms(
            user_cube, moving, rating, packed, row_index, col_index
        )
        carried = shifted(carried + item_increment, "item", 1)
        moving = shifted(moving, "item", 1)
        return (moving, carried, user_grad + user_increment)

    carried_start = jnp.zeros((rank_len, shard_len), jnp.float32)
    _, carried, user_grad = lax.fori_loop(
        0, cycle_size, cycle_step, (item_factors, carried_start, user_start)
    )
    user_total = lax.psum(user_grad, "layer")
    item_total = lax.psum(carried, ("user", "layer"))
    grad_users = LOSS_SCALE * user_total + DECAY * user_factors.astype(jnp.float32)
    grad_items = LOSS_SCALE * item_total + DECAY * item_factors.astype(jnp.float32)
    return (grad_users, grad_items)


def solution(mesh):
    return jax.shard_map(
        body,
        mesh=mesh,
        in_specs=(
            P(None, ("user", "item")),
            P(None, "item"),
            P(("user", "item", "layer"), None, None),
            P(("user", "item", "layer"), None, None),
            P(("user", "item", "layer")),
            P(("user", "item", "layer")),
        ),
        out_specs=(P(None, ("user", "item")), P(None, "item")),
        check_vma=False,
    )
```

profile of v0, /device:TPU:1, one launch (start us, length us, event | category | flops | bytes accessed | tf_op | source)
XLA Modules:
  0.0 713.4 jit_solution(4135386083093279149)
XLA Ops:
  9.0 304.6 %while.20 = (s32[]{:T(128)}, bf16[64,1024]{1,0:T(8,128)(2,1)S(1)}, f32[64,1024]{1,0:T(8,128)S(1)}, f32[64,512]{1,0:T(8,128)S(1)}, s32[]{:T(128)}, /*index=5*/s32...) while((s32[]{:T(128)}, bf16[64,1024]{1,0:T(8,128)(2,1)S(1)}, ...), condition=%wide.region_1.2_spmd.clone, body=%wide.region_0.1_spmd.clone.sunk | while | flops 62521552 | bytes 6949542 | solution.py:94
  9.1 4.5 collective-permute-start
  16.5 1.3 fusion.69
  18.5 3.5 collective-permute-start.1
  22.8 6.7 collective-permute-done.1
  29.5 1.9 collective-permute-start
  34.3 1.3 fusion.69
  36.3 2.9 collective-permute-start.1
  39.9 8.0 %collective-permute-done.1 = f32[64,1024]{1,0:T(8,128)S(1)} collective-permute-done((f32[64,1024]{1,0:T(8,128)S(1)}, f32[64,1024]{1,0:T(8,128)S(1)}, u32[]{:S(2)}, u32[]{:S(2)}) %collective-permute-start.1) | collective-permute-done | bytes 262176 | tf_op jit(solution)/shard_map/while/body/eval_jaxpr/ppermute | solution.py:13
  48.0 1.9 collective-permute-start
  52.8 1.3 fusion.69
  54.8 1.9 collective-permute-start.1
  57.6 9.3 %collective-permute-done.1 = f32[64,1024]{1,0:T(8,128)S(1)} collective-permute-done((f32[64,1024]{1,0:T(8,128)S(1)}, f32[64,1024]{1,0:T(8,128)S(1)}, u32[]{:S(2)}, u32[]{:S(2)}) %collective-permute-start.1) | collective-permute-done | bytes 262176 | tf_op jit(solution)/shard_map/while/body/eval_jaxpr/ppermute | solution.py:13
  67.0 1.9 collective-permute-start
  71.8 1.3 fusion.69
  73.7 1.9 collective-permute-start.1
  76.6 9.3 %collective-permute-done.1 = f32[64,1024]{1,0:T(8,128)S(1)} collective-permute-done((f32[64,1024]{1,0:T(8,128)S(1)}, f32[64,1024]{1,0:T(8,128)S(1)}, u32[]{:S(2)}, u32[]{:S(2)}) %collective-permute-start.1) | collective-permute-done | bytes 262176 | tf_op jit(solution)/shard_map/while/body/eval_jaxpr/ppermute | solution.py:13
  85.9 1.9 collective-permute-start
  90.8 1.3 fusion.69
  92.7 1.9 collective-permute-start.1
  95.6 9.3 %collective-permute-done.1 = f32[64,1024]{1,0:T(8,128)S(1)} collective-permute-done((f32[64,1024]{1,0:T(8,128)S(1)}, f32[64,1024]{1,0:T(8,128)S(1)}, u32[]{:S(2)}, u32[]{:S(2)}) %collective-permute-start.1) | collective-permute-done | bytes 262176 | tf_op jit(solution)/shard_map/while/body/eval_jaxpr/ppermute | solution.py:13
  104.9 1.9 collective-permute-start
  109.8 1.3 fusion.69
  111.7 1.9 collective-permute-start.1
  114.5 9.3 %collective-permute-done.1 = f32[64,1024]{1,0:T(8,128)S(1)} collective-permute-done((f32[64,1024]{1,0:T(8,128)S(1)}, f32[64,1024]{1,0:T(8,128)S(1)}, u32[]{:S(2)}, u32[]{:S(2)}) %collective-permute-start.1) | collective-permute-done | bytes 262176 | tf_op jit(solution)/shard_map/while/body/eval_jaxpr/ppermute | solution.py:13
  123.9 1.9 collective-permute-start
  128.7 1.3 fusion.69
  130.7 1.9 collective-permute-start.1
  133.5 9.3 %collective-permute-done.1 = f32[64,1024]{1,0:T(8,128)S(1)} collective-permute-done((f32[64,1024]{1,0:T(8,128)S(1)}, f32[64,1024]{1,0:T(8,128)S(1)}, u32[]{:S(2)}, u32[]{:S(2)}) %collective-permute-start.1) | collective-permute-done | bytes 262176 | tf_op jit(solution)/shard_map/while/body/eval_jaxpr/ppermute | solution.py:13
  142.9 1.9 collective-permute-start
  147.7 1.3 fusion.69
  149.7 1.9 collective-permute-start.1
  152.5 9.3 %collective-permute-done.1 = f32[64,1024]{1,0:T(8,128)S(1)} collective-permute-done((f32[64,1024]{1,0:T(8,128)S(1)}, f32[64,1024]{1,0:T(8,128)S(1)}, u32[]{:S(2)}, u32[]{:S(2)}) %collective-permute-start.1) | collective-permute-done | bytes 262176 | tf_op jit(solution)/shard_map/while/body/eval_jaxpr/ppermute | solution.py:13
  161.9 1.9 collective-permute-start
  166.7 1.3 fusion.69
  168.6 1.9 collective-permute-start.1
  171.5 9.3 %collective-permute-done.1 = f32[64,1024]{1,0:T(8,128)S(1)} collective-permute-done((f32[64,1024]{1,0:T(8,128)S(1)}, f32[64,1024]{1,0:T(8,128)S(1)}, u32[]{:S(2)}, u32[]{:S(2)}) %collective-permute-start.1) | collective-permute-done | bytes 262176 | tf_op jit(solution)/shard_map/while/body/eval_jaxpr/ppermute | solution.py:13
  180.8 1.9 collective-permute-start
  185.7 1.3 fusion.69
  187.6 1.9 collective-permute-start.1
  190.5 9.3 %collective-permute-done.1 = f32[64,1024]{1,0:T(8,128)S(1)} collective-permute-done((f32[64,1024]{1,0:T(8,128)S(1)}, f32[64,1024]{1,0:T(8,128)S(1)}, u32[]{:S(2)}, u32[]{:S(2)}) %collective-permute-start.1) | collective-permute-done | bytes 262176 | tf_op jit(solution)/shard_map/while/body/eval_jaxpr/ppermute | solution.py:13
  199.8 1.9 collective-permute-start
  206.6 1.9 collective-permute-start.1
  209.4 9.3 %collective-permute-done.1 = f32[64,1024]{1,0:T(8,128)S(1)} collective-permute-done((f32[64,1024]{1,0:T(8,128)S(1)}, f32[64,1024]{1,0:T(8,128)S(1)}, u32[]{:S(2)}, u32[]{:S(2)}) %collective-permute-start.1) | collective-permute-done | bytes 262176 | tf_op jit(solution)/shard_map/while/body/eval_jaxpr/ppermute | solution.py:13
  218.8 1.9 collective-permute-start
  223.7 1.3 fusion.69
  225.6 1.9 collective-permute-start.1
  228.4 9.3 %collective-permute-done.1 = f32[64,1024]{1,0:T(8,128)S(1)} collective-permute-done((f32[64,1024]{1,0:T(8,128)S(1)}, f32[64,1024]{1,0:T(8,128)S(1)}, u32[]{:S(2)}, u32[]{:S(2)}) %collective-permute-start.1) | collective-permute-done | bytes 262176 | tf_op jit(solution)/shard_map/while/body/eval_jaxpr/ppermute | solution.py:13
  237.8 1.9 collective-permute-start
  244.6 1.9 collective-permute-start.1
  247.4 9.3 %collective-permute-done.1 = f32[64,1024]{1,0:T(8,128)S(1)} collective-permute-done((f32[64,1024]{1,0:T(8,128)S(1)}, f32[64,1024]{1,0:T(8,128)S(1)}, u32[]{:S(2)}, u32[]{:S(2)}) %collective-permute-start.1) | collective-permute-done | bytes 262176 | tf_op jit(solution)/shard_map/while/body/eval_jaxpr/ppermute | solution.py:13
  256.8 1.9 collective-permute-start
  263.6 1.9 collective-permute-start.1
  266.4 9.3 %collective-permute-done.1 = f32[64,1024]{1,0:T(8,128)S(1)} collective-permute-done((f32[64,1024]{1,0:T(8,128)S(1)}, f32[64,1024]{1,0:T(8,128)S(1)}, u32[]{:S(2)}, u32[]{:S(2)}) %collective-permute-start.1) | collective-permute-done | bytes 262176 | tf_op jit(solution)/shard_map/while/body/eval_jaxpr/ppermute | solution.py:13
  275.7 1.9 collective-permute-start
  282.5 1.9 collective-permute-start.1
  285.4 9.3 %collective-permute-done.1 = f32[64,1024]{1,0:T(8,128)S(1)} collective-permute-done((f32[64,1024]{1,0:T(8,128)S(1)}, f32[64,1024]{1,0:T(8,128)S(1)}, u32[]{:S(2)}, u32[]{:S(2)}) %collective-permute-start.1) | collective-permute-done | bytes 262176 | tf_op jit(solution)/shard_map/while/body/eval_jaxpr/ppermute | solution.py:13
  294.7 1.9 collective-permute-start
  301.5 1.9 collective-permute-start.1
  304.3 9.3 %collective-permute-done.1 = f32[64,1024]{1,0:T(8,128)S(1)} collective-permute-done((f32[64,1024]{1,0:T(8,128)S(1)}, f32[64,1024]{1,0:T(8,128)S(1)}, u32[]{:S(2)}, u32[]{:S(2)}) %collective-permute-start.1) | collective-permute-done | bytes 262176 | tf_op jit(solution)/shard_map/while/body/eval_jaxpr/ppermute | solution.py:13
  315.1 44.8 %all-reduce.3.cloned.1.call-done = f32[64,512]{1,0:T(8,128)} async-done(((f32[64,512]{1,0:T(8,128)}), f32[64,512]{1,0:T(8,128)}) %all-reduce.3.cloned.1.call-update) | async-done | bytes 131088 | tf_op jit(solution)/shard_map/psum | solution.py:97
  359.9 1.6 multiply_add_fusion.1
  361.5 343.4 %all-reduce.5.cloned.1.call-done = f32[64,1024]{1,0:T(8,128)} async-done(((f32[64,1024]{1,0:T(8,128)}), f32[64,1024]{1,0:T(8,128)}) %all-reduce.5.cloned.1.call-update) | async-done | bytes 262160 | tf_op jit(solution)/shard_map/psum | solution.py:98
  704.9 1.7 multiply_add_fusion
  (277 shorter events, 80.0 us)
Async XLA Ops:
  7.2 352.7 %all-reduce.3.cloned.1.call-start = ((), (), s32[]{:S(2)}) async-start(), calls=%async_computation | async-start | bytes 262144 | tf_op jit(solution)/shard_map/psum | solution.py:97
  9.0 350.9 %copy-start.3 = (bf16[64,512]{1,0:T(8,128)(2,1)S(1)}, bf16[64,512]{1,0:T(8,128)(2,1)}, u32[]{:S(2)}) copy-start(bf16[64,512]{1,0:T(8,128)(2,1)} %param.8) | copy-start | bytes 196612
  9.0 695.8 %copy-start.2 = (bf16[64,1024]{1,0:T(8,128)(2,1)S(1)}, bf16[64,1024]{1,0:T(8,128)(2,1)}, u32[]{:S(2)}) copy-start(bf16[64,1024]{1,0:T(8,128)(2,1)} %param.9) | copy-start | bytes 393220
  9.1 13.7 %collective-permute-start = (bf16[64,1024]{1,0:T(8,128)(2,1)S(1)}, bf16[64,1024]{1,0:T(8,128)(2,1)S(1)}, u32[]{:S(2)}, u32[]{:S(2)}) collective-permute-start(bf16[64,1024]{1,0:T(8,128)(2,1)S(1)} %copy.62), channel_id=1, source_target_pairs={{30,0},{0,2},{2,4},{4,6},{6,8},{8,10},{10,12},{12,14},{14,16},{16,... | collective-permute-start | bytes 393224 | tf_op jit(solution)/shard_map/while/body/eval_jaxpr/ppermute | solution.py:13
  18.5 11.0 %collective-permute-start.1 = (f32[64,1024]{1,0:T(8,128)S(1)}, f32[64,1024]{1,0:T(8,128)S(1)}, u32[]{:S(2)}, u32[]{:S(2)}) collective-permute-start(f32[64,1024]{1,0:T(8,128)S(1)} %bitcast_add_fusion.4), channel_id=1, source_target_pairs={{30,0},{0,2},{2,4},{4,6},{6,8},{8,10},{10,12},{12,14},{14,16},{16,... | collective-permute-start | bytes 786440 | tf_op jit(solution)/shard_map/while/body/eval_jaxpr/ppermute | solution.py:13
  29.5 10.4 %collective-permute-start = (bf16[64,1024]{1,0:T(8,128)(2,1)S(1)}, bf16[64,1024]{1,0:T(8,128)(2,1)S(1)}, u32[]{:S(2)}, u32[]{:S(2)}) collective-permute-start(bf16[64,1024]{1,0:T(8,128)(2,1)S(1)} %copy.62), channel_id=1, source_target_pairs={{30,0},{0,2},{2,4},{4,6},{6,8},{8,10},{10,12},{12,14},{14,16},{16,... | collective-permute-start | bytes 393224 | tf_op jit(solution)/shard_map/while/body/eval_jaxpr/ppermute | solution.py:13
  36.3 11.7 %collective-permute-start.1 = (f32[64,1024]{1,0:T(8,128)S(1)}, f32[64,1024]{1,0:T(8,128)S(1)}, u32[]{:S(2)}, u32[]{:S(2)}) collective-permute-start(f32[64,1024]{1,0:T(8,128)S(1)} %bitcast_add_fusion.4), channel_id=1, source_target_pairs={{30,0},{0,2},{2,4},{4,6},{6,8},{8,10},{10,12},{12,14},{14,16},{16,... | collective-permute-start | bytes 786440 | tf_op jit(solution)/shard_map/while/body/eval_jaxpr/ppermute | solution.py:13
  48.0 9.6 %collective-permute-start = (bf16[64,1024]{1,0:T(8,128)(2,1)S(1)}, bf16[64,1024]{1,0:T(8,128)(2,1)S(1)}, u32[]{:S(2)}, u32[]{:S(2)}) collective-permute-start(bf16[64,1024]{1,0:T(8,128)(2,1)S(1)} %copy.62), channel_id=1, source_target_pairs={{30,0},{0,2},{2,4},{4,6},{6,8},{8,10},{10,12},{12,14},{14,16},{16,... | collective-permute-start | bytes 393224 | tf_op jit(solution)/shard_map/while/body/eval_jaxpr/ppermute | solution.py:13
  54.8 12.2 %collective-permute-start.1 = (f32[64,1024]{1,0:T(8,128)S(1)}, f32[64,1024]{1,0:T(8,128)S(1)}, u32[]{:S(2)}, u32[]{:S(2)}) collective-permute-start(f32[64,1024]{1,0:T(8,128)S(1)} %bitcast_add_fusion.4), channel_id=1, source_target_pairs={{30,0},{0,2},{2,4},{4,6},{6,8},{8,10},{10,12},{12,14},{14,16},{16,... | collective-permute-start | bytes 786440 | tf_op jit(solution)/shard_map/while/body/eval_jaxpr/ppermute | solution.py:13
  67.0 9.6 %collective-permute-start = (bf16[64,1024]{1,0:T(8,128)(2,1)S(1)}, bf16[64,1024]{1,0:T(8,128)(2,1)S(1)}, u32[]{:S(2)}, u32[]{:S(2)}) collective-permute-start(bf16[64,1024]{1,0:T(8,128)(2,1)S(1)} %copy.62), channel_id=1, source_target_pairs={{30,0},{0,2},{2,4},{4,6},{6,8},{8,10},{10,12},{12,14},{14,16},{16,... | collective-permute-start | bytes 393224 | tf_op jit(solution)/shard_map/while/body/eval_jaxpr/ppermute | solution.py:13
  73.7 12.2 %collective-permute-start.1 = (f32[64,1024]{1,0:T(8,128)S(1)}, f32[64,1024]{1,0:T(8,128)S(1)}, u32[]{:S(2)}, u32[]{:S(2)}) collective-permute-start(f32[64,1024]{1,0:T(8,128)S(1)} %bitcast_add_fusion.4), channel_id=1, source_target_pairs={{30,0},{0,2},{2,4},{4,6},{6,8},{8,10},{10,12},{12,14},{14,16},{16,... | collective-permute-start | bytes 786440 | tf_op jit(solution)/shard_map/while/body/eval_jaxpr/ppermute | solution.py:13
  85.9 9.6 %collective-permute-start = (bf16[64,1024]{1,0:T(8,128)(2,1)S(1)}, bf16[64,1024]{1,0:T(8,128)(2,1)S(1)}, u32[]{:S(2)}, u32[]{:S(2)}) collective-permute-start(bf16[64,1024]{1,0:T(8,128)(2,1)S(1)} %copy.62), channel_id=1, source_target_pairs={{30,0},{0,2},{2,4},{4,6},{6,8},{8,10},{10,12},{12,14},{14,16},{16,... | collective-permute-start | bytes 393224 | tf_op jit(solution)/shard_map/while/body/eval_jaxpr/ppermute | solution.py:13
  92.7 12.2 %collective-permute-start.1 = (f32[64,1024]{1,0:T(8,128)S(1)}, f32[64,1024]{1,0:T(8,128)S(1)}, u32[]{:S(2)}, u32[]{:S(2)}) collective-permute-start(f32[64,1024]{1,0:T(8,128)S(1)} %bitcast_add_fusion.4), channel_id=1, source_target_pairs={{30,0},{0,2},{2,4},{4,6},{6,8},{8,10},{10,12},{12,14},{14,16},{16,... | collective-permute-start | bytes 786440 | tf_op jit(solution)/shard_map/while/body/eval_jaxpr/ppermute | solution.py:13
  104.9 9.6 %collective-permute-start = (bf16[64,1024]{1,0:T(8,128)(2,1)S(1)}, bf16[64,1024]{1,0:T(8,128)(2,1)S(1)}, u32[]{:S(2)}, u32[]{:S(2)}) collective-permute-start(bf16[64,1024]{1,0:T(8,128)(2,1)S(1)} %copy.62), channel_id=1, source_target_pairs={{30,0},{0,2},{2,4},{4,6},{6,8},{8,10},{10,12},{12,14},{14,16},{16,... | collective-permute-start | bytes 393224 | tf_op jit(solution)/shard_map/while/body/eval_jaxpr/ppermute | solution.py:13
  111.7 12.2 %collective-permute-start.1 = (f32[64,1024]{1,0:T(8,128)S(1)}, f32[64,1024]{1,0:T(8,128)S(1)}, u32[]{:S(2)}, u32[]{:S(2)}) collective-permute-start(f32[64,1024]{1,0:T(8,128)S(1)} %bitcast_add_fusion.4), channel_id=1, source_target_pairs={{30,0},{0,2},{2,4},{4,6},{6,8},{8,10},{10,12},{12,14},{14,16},{16,... | collective-permute-start | bytes 786440 | tf_op jit(solution)/shard_map/while/body/eval_jaxpr/ppermute | solution.py:13
  123.9 9.6 %collective-permute-start = (bf16[64,1024]{1,0:T(8,128)(2,1)S(1)}, bf16[64,1024]{1,0:T(8,128)(2,1)S(1)}, u32[]{:S(2)}, u32[]{:S(2)}) collective-permute-start(bf16[64,1024]{1,0:T(8,128)(2,1)S(1)} %copy.62), channel_id=1, source_target_pairs={{30,0},{0,2},{2,4},{4,6},{6,8},{8,10},{10,12},{12,14},{14,16},{16,... | collective-permute-start | bytes 393224 | tf_op jit(solution)/shard_map/while/body/eval_jaxpr/ppermute | solution.py:13
  130.7 12.2 %collective-permute-start.1 = (f32[64,1024]{1,0:T(8,128)S(1)}, f32[64,1024]{1,0:T(8,128)S(1)}, u32[]{:S(2)}, u32[]{:S(2)}) collective-permute-start(f32[64,1024]{1,0:T(8,128)S(1)} %bitcast_add_fusion.4), channel_id=1, source_target_pairs={{30,0},{0,2},{2,4},{4,6},{6,8},{8,10},{10,12},{12,14},{14,16},{16,... | collective-permute-start | bytes 786440 | tf_op jit(solution)/shard_map/while/body/eval_jaxpr/ppermute | solution.py:13
  142.9 9.6 %collective-permute-start = (bf16[64,1024]{1,0:T(8,128)(2,1)S(1)}, bf16[64,1024]{1,0:T(8,128)(2,1)S(1)}, u32[]{:S(2)}, u32[]{:S(2)}) collective-permute-start(bf16[64,1024]{1,0:T(8,128)(2,1)S(1)} %copy.62), channel_id=1, source_target_pairs={{30,0},{0,2},{2,4},{4,6},{6,8},{8,10},{10,12},{12,14},{14,16},{16,... | collective-permute-start | bytes 393224 | tf_op jit(solution)/shard_map/while/body/eval_jaxpr/ppermute | solution.py:13
  149.7 12.2 %collective-permute-start.1 = (f32[64,1024]{1,0:T(8,128)S(1)}, f32[64,1024]{1,0:T(8,128)S(1)}, u32[]{:S(2)}, u32[]{:S(2)}) collective-permute-start(f32[64,1024]{1,0:T(8,128)S(1)} %bitcast_add_fusion.4), channel_id=1, source_target_pairs={{30,0},{0,2},{2,4},{4,6},{6,8},{8,10},{10,12},{12,14},{14,16},{16,... | collective-permute-start | bytes 786440 | tf_op jit(solution)/shard_map/while/body/eval_jaxpr/ppermute | solution.py:13
  161.9 9.6 %collective-permute-start = (bf16[64,1024]{1,0:T(8,128)(2,1)S(1)}, bf16[64,1024]{1,0:T(8,128)(2,1)S(1)}, u32[]{:S(2)}, u32[]{:S(2)}) collective-permute-start(bf16[64,1024]{1,0:T(8,128)(2,1)S(1)} %copy.62), channel_id=1, source_target_pairs={{30,0},{0,2},{2,4},{4,6},{6,8},{8,10},{10,12},{12,14},{14,16},{16,... | collective-permute-start | bytes 393224 | tf_op jit(solution)/shard_map/while/body/eval_jaxpr/ppermute | solution.py:13
  168.6 12.2 %collective-permute-start.1 = (f32[64,1024]{1,0:T(8,128)S(1)}, f32[64,1024]{1,0:T(8,128)S(1)}, u32[]{:S(2)}, u32[]{:S(2)}) collective-permute-start(f32[64,1024]{1,0:T(8,128)S(1)} %bitcast_add_fusion.4), channel_id=1, source_target_pairs={{30,0},{0,2},{2,4},{4,6},{6,8},{8,10},{10,12},{12,14},{14,16},{16,... | collective-permute-start | bytes 786440 | tf_op jit(solution)/shard_map/while/body/eval_jaxpr/ppermute | solution.py:13
  180.8 9.6 %collective-permute-start = (bf16[64,1024]{1,0:T(8,128)(2,1)S(1)}, bf16[64,1024]{1,0:T(8,128)(2,1)S(1)}, u32[]{:S(2)}, u32[]{:S(2)}) collective-permute-start(bf16[64,1024]{1,0:T(8,128)(2,1)S(1)} %copy.62), channel_id=1, source_target_pairs={{30,0},{0,2},{2,4},{4,6},{6,8},{8,10},{10,12},{12,14},{14,16},{16,... | collective-permute-start | bytes 393224 | tf_op jit(solution)/shard_map/while/body/eval_jaxpr/ppermute | solution.py:13
  187.6 12.2 %collective-permute-start.1 = (f32[64,1024]{1,0:T(8,128)S(1)}, f32[64,1024]{1,0:T(8,128)S(1)}, u32[]{:S(2)}, u32[]{:S(2)}) collective-permute-start(f32[64,1024]{1,0:T(8,128)S(1)} %bitcast_add_fusion.4), channel_id=1, source_target_pairs={{30,0},{0,2},{2,4},{4,6},{6,8},{8,10},{10,12},{12,14},{14,16},{16,... | collective-permute-start | bytes 786440 | tf_op jit(solution)/shard_map/while/body/eval_jaxpr/ppermute | solution.py:13
  199.8 9.6 %collective-permute-start = (bf16[64,1024]{1,0:T(8,128)(2,1)S(1)}, bf16[64,1024]{1,0:T(8,128)(2,1)S(1)}, u32[]{:S(2)}, u32[]{:S(2)}) collective-permute-start(bf16[64,1024]{1,0:T(8,128)(2,1)S(1)} %copy.62), channel_id=1, source_target_pairs={{30,0},{0,2},{2,4},{4,6},{6,8},{8,10},{10,12},{12,14},{14,16},{16,... | collective-permute-start | bytes 393224 | tf_op jit(solution)/shard_map/while/body/eval_jaxpr/ppermute | solution.py:13
  206.6 12.2 %collective-permute-start.1 = (f32[64,1024]{1,0:T(8,128)S(1)}, f32[64,1024]{1,0:T(8,128)S(1)}, u32[]{:S(2)}, u32[]{:S(2)}) collective-permute-start(f32[64,1024]{1,0:T(8,128)S(1)} %bitcast_add_fusion.4), channel_id=1, source_target_pairs={{30,0},{0,2},{2,4},{4,6},{6,8},{8,10},{10,12},{12,14},{14,16},{16,... | collective-permute-start | bytes 786440 | tf_op jit(solution)/shard_map/while/body/eval_jaxpr/ppermute | solution.py:13
  218.8 9.6 %collective-permute-start = (bf16[64,1024]{1,0:T(8,128)(2,1)S(1)}, bf16[64,1024]{1,0:T(8,128)(2,1)S(1)}, u32[]{:S(2)}, u32[]{:S(2)}) collective-permute-start(bf16[64,1024]{1,0:T(8,128)(2,1)S(1)} %copy.62), channel_id=1, source_target_pairs={{30,0},{0,2},{2,4},{4,6},{6,8},{8,10},{10,12},{12,14},{14,16},{16,... | collective-permute-start | bytes 393224 | tf_op jit(solution)/shard_map/while/body/eval_jaxpr/ppermute | solution.py:13
  225.6 12.2 %collective-permute-start.1 = (f32[64,1024]{1,0:T(8,128)S(1)}, f32[64,1024]{1,0:T(8,128)S(1)}, u32[]{:S(2)}, u32[]{:S(2)}) collective-permute-start(f32[64,1024]{1,0:T(8,128)S(1)} %bitcast_add_fusion.4), channel_id=1, source_target_pairs={{30,0},{0,2},{2,4},{4,6},{6,8},{8,10},{10,12},{12,14},{14,16},{16,... | collective-permute-start | bytes 786440 | tf_op jit(solution)/shard_map/while/body/eval_jaxpr/ppermute | solution.py:13
  237.8 9.6 %collective-permute-start = (bf16[64,1024]{1,0:T(8,128)(2,1)S(1)}, bf16[64,1024]{1,0:T(8,128)(2,1)S(1)}, u32[]{:S(2)}, u32[]{:S(2)}) collective-permute-start(bf16[64,1024]{1,0:T(8,128)(2,1)S(1)} %copy.62), channel_id=1, source_target_pairs={{30,0},{0,2},{2,4},{4,6},{6,8},{8,10},{10,12},{12,14},{14,16},{16,... | collective-permute-start | bytes 393224 | tf_op jit(solution)/shard_map/while/body/eval_jaxpr/ppermute | solution.py:13
  244.6 12.2 %collective-permute-start.1 = (f32[64,1024]{1,0:T(8,128)S(1)}, f32[64,1024]{1,0:T(8,128)S(1)}, u32[]{:S(2)}, u32[]{:S(2)}) collective-permute-start(f32[64,1024]{1,0:T(8,128)S(1)} %bitcast_add_fusion.4), channel_id=1, source_target_pairs={{30,0},{0,2},{2,4},{4,6},{6,8},{8,10},{10,12},{12,14},{14,16},{16,... | collective-permute-start | bytes 786440 | tf_op jit(solution)/shard_map/while/body/eval_jaxpr/ppermute | solution.py:13
  256.8 9.6 %collective-permute-start = (bf16[64,1024]{1,0:T(8,128)(2,1)S(1)}, bf16[64,1024]{1,0:T(8,128)(2,1)S(1)}, u32[]{:S(2)}, u32[]{:S(2)}) collective-permute-start(bf16[64,1024]{1,0:T(8,128)(2,1)S(1)} %copy.62), channel_id=1, source_target_pairs={{30,0},{0,2},{2,4},{4,6},{6,8},{8,10},{10,12},{12,14},{14,16},{16,... | collective-permute-start | bytes 393224 | tf_op jit(solution)/shard_map/while/body/eval_jaxpr/ppermute | solution.py:13
  263.6 12.2 %collective-permute-start.1 = (f32[64,1024]{1,0:T(8,128)S(1)}, f32[64,1024]{1,0:T(8,128)S(1)}, u32[]{:S(2)}, u32[]{:S(2)}) collective-permute-start(f32[64,1024]{1,0:T(8,128)S(1)} %bitcast_add_fusion.4), channel_id=1, source_target_pairs={{30,0},{0,2},{2,4},{4,6},{6,8},{8,10},{10,12},{12,14},{14,16},{16,... | collective-permute-start | bytes 786440 | tf_op jit(solution)/shard_map/while/body/eval_jaxpr/ppermute | solution.py:13
  275.7 9.6 %collective-permute-start = (bf16[64,1024]{1,0:T(8,128)(2,1)S(1)}, bf16[64,1024]{1,0:T(8,128)(2,1)S(1)}, u32[]{:S(2)}, u32[]{:S(2)}) collective-permute-start(bf16[64,1024]{1,0:T(8,128)(2,1)S(1)} %copy.62), channel_id=1, source_target_pairs={{30,0},{0,2},{2,4},{4,6},{6,8},{8,10},{10,12},{12,14},{14,16},{16,... | collective-permute-start | bytes 393224 | tf_op jit(solution)/shard_map/while/body/eval_jaxpr/ppermute | solution.py:13
  282.5 12.2 %collective-permute-start.1 = (f32[64,1024]{1,0:T(8,128)S(1)}, f32[64,1024]{1,0:T(8,128)S(1)}, u32[]{:S(2)}, u32[]{:S(2)}) collective-permute-start(f32[64,1024]{1,0:T(8,128)S(1)} %bitcast_add_fusion.4), channel_id=1, source_target_pairs={{30,0},{0,2},{2,4},{4,6},{6,8},{8,10},{10,12},{12,14},{14,16},{16,... | collective-permute-start | bytes 786440 | tf_op jit(solution)/shard_map/while/body/eval_jaxpr/ppermute | solution.py:13
  294.7 9.6 %collective-permute-start = (bf16[64,1024]{1,0:T(8,128)(2,1)S(1)}, bf16[64,1024]{1,0:T(8,128)(2,1)S(1)}, u32[]{:S(2)}, u32[]{:S(2)}) collective-permute-start(bf16[64,1024]{1,0:T(8,128)(2,1)S(1)} %copy.62), channel_id=1, source_target_pairs={{30,0},{0,2},{2,4},{4,6},{6,8},{8,10},{10,12},{12,14},{14,16},{16,... | collective-permute-start | bytes 393224 | tf_op jit(solution)/shard_map/while/body/eval_jaxpr/ppermute | solution.py:13
  301.5 12.2 %collective-permute-start.1 = (f32[64,1024]{1,0:T(8,128)S(1)}, f32[64,1024]{1,0:T(8,128)S(1)}, u32[]{:S(2)}, u32[]{:S(2)}) collective-permute-start(f32[64,1024]{1,0:T(8,128)S(1)} %bitcast_add_fusion.4), channel_id=1, source_target_pairs={{30,0},{0,2},{2,4},{4,6},{6,8},{8,10},{10,12},{12,14},{14,16},{16,... | collective-permute-start | bytes 786440 | tf_op jit(solution)/shard_map/while/body/eval_jaxpr/ppermute | solution.py:13
  313.7 0.7 copy-start.1
  313.7 0.7 copy-start
  314.4 390.5 %all-reduce.5.cloned.1.call-start = ((), (), s32[]{:S(2)}) async-start(), calls=%async_computation.1 | async-start | bytes 524288 | tf_op jit(solution)/shard_map/psum | solution.py:98
Sparse Core Ops, SparseCore 0:
  314.5 45.3 all-reduce.2
  363.4 341.4 all-reduce.4
where the time goes:
time: 716 us; the launch traced here: 713 us
  waiting for transfers between devices  537 us (75%)
  starting transfers between devices  66.7 us (9%)
  matrix products  47.9 us (7%)
  local copies, waits for them, and re-layouts  41.2 us (6%)
  between operations  14.1 us (2%)
    psum x1, waiting for transfers between devices, body(): item_total = lax.psum(carried, ('user', 'layer'))  343 us
    ppermute x32, waiting for transfers between devices, shifted(): return lax.ppermute(block, axis, route)  148 us
    ppermute x32, starting transfers between devices, shifted(): return lax.ppermute(block, axis, route)  66.6 us
    psum x1, waiting for transfers between devices, body(): user_total = lax.psum(user_grad, 'layer')  44.8 us
    dot_general x16, matrix products, shard_terms(): jnp.einsum('bjy,bjf->jyf', user_portion, item_portion, preferred_element_...  20.1 us
  transfers between devices with their start and end apart: 34, of which 32 were waited for; matrix products, arithmetic and copies ran while one was open for 13% of the time, Pallas kernels for 0%

commit v1 on v0

v1 whole, which is shorter than its diff:
```python
import jax
import jax.numpy as jnp
from jax import lax
from jax.experimental import pallas as pl
from jax.experimental.pallas import tpu as pltpu
from jax.sharding import Mesh
from jax.sharding import PartitionSpec as P

LOSS_SCALE = 0.0625
DECAY = 0.1
TB = 128
SIDE = 4
BF16 = jnp.bfloat16
F32 = jnp.float32


def tile_kernel(
    rows_ref, cols_ref, layer_ref, user_ref, own_ref, other_ref, rating_ref, mask_ref,
    keep_ref, send_ref, user_out_ref, user_t_ref, item_acc_ref,
):
    step = pl.program_id(0)
    layer = layer_ref[0]
    per_shard = rating_ref.shape[0]
    user_blocks = user_out_ref.shape[0]
    half_blocks = own_ref.shape[1]

    @pl.when(step == 0)
    def _():
        user_out_ref[...] = jnp.zeros_like(user_out_ref)
        for b in range(user_blocks):
            block = user_ref[:, b * TB:(b + 1) * TB].astype(F32)
            user_t_ref[b] = block.T.astype(BF16)

    item_acc_ref[...] = jnp.zeros_like(item_acc_ref)
    bit = jnp.left_shift(jnp.int32(1), lax.broadcasted_iota(jnp.int32, (8, TB), 0))
    words = mask_ref.shape[1]
    increments = []
    for t in range(per_shard):
        b = rows_ref[step * per_shard + t]
        c = cols_ref[step * per_shard + t]
        place = c % half_blocks
        item = jnp.where(c // half_blocks == layer, own_ref[0, place], other_ref[0, place])
        scores = jnp.dot(user_t_ref[b], item, preferred_element_type=F32)
        difference = scores - rating_ref[t].astype(F32)
        parts = []
        for w in range(words):
            word = jnp.broadcast_to(mask_ref[t, w:w + 1, :], (8, TB))
            parts.append(jnp.where((word & bit) != 0, difference[w * 8:(w + 1) * 8], 0.0))
        residual = jnp.concatenate(parts, axis=0).astype(BF16)
        user = user_ref[:, pl.ds(pl.multiple_of(b * TB, TB), TB)]
        item_inc = jnp.dot(user, residual, preferred_element_type=F32)
        user_inc = lax.dot_general(
            item, residual, (((1,), (1,)), ((), ())), preferred_element_type=F32
        )
        increments.append((b, c, user_inc, item_inc))
    for b, c, user_inc, item_inc in increments:
        user_out_ref[b] += user_inc
        item_acc_ref[c] += item_inc
    for j in range(half_blocks):
        keep_ref[0, j] = item_acc_ref[layer * half_blocks + j].astype(BF16)
        send_ref[0, j] = item_acc_ref[(1 - layer) * half_blocks + j].astype(BF16)


def tile_terms(rows, cols, layer, user_factors, own, other, ratings, masks):
    shards, half_blocks, rank, _ = own.shape
    per_shard = ratings.shape[0] // shards
    user_blocks = user_factors.shape[1] // TB
    words = masks.shape[1]
    half = pl.BlockSpec((1, half_blocks, rank, TB), lambda i, *_: (i, 0, 0, 0))
    return pl.pallas_call(
        tile_kernel,
        grid_spec=pltpu.PrefetchScalarGridSpec(
            num_scalar_prefetch=3,
            grid=(shards,),
            in_specs=[
                pl.BlockSpec(user_factors.shape, lambda i, *_: (0, 0)),
                half,
                half,
                pl.BlockSpec((per_shard, TB, TB), lambda i, *_: (i, 0, 0)),
                pl.BlockSpec((per_shard, words, TB), lambda i, *_: (i, 0, 0)),
            ],
            out_specs=[
                half,
                half,
                pl.BlockSpec((user_blocks, rank, TB), lambda i, *_: (0, 0, 0)),
            ],
            scratch_shapes=[
                pltpu.VMEM((user_blocks, TB, rank), BF16),
                pltpu.VMEM((2 * half_blocks, rank, TB), F32),
            ],
        ),
        out_shape=[
            jax.ShapeDtypeStruct(own.shape, BF16),
            jax.ShapeDtypeStruct(own.shape, BF16),
            jax.ShapeDtypeStruct((user_blocks, rank, TB), F32),
        ],
        compiler_params=pltpu.CompilerParams(vmem_limit_bytes=32 * 1024 * 1024),
        name="tile_terms",
    )(rows, cols, layer, user_factors, own, other, ratings, masks)


def spread(block, axis):
    copies = jnp.broadcast_to(block[None], (SIDE,) + block.shape)
    return lax.all_to_all(copies, axis, 0, 0)


def body(user_factors, item_factors, ratings, masks, tile_rows, tile_cols):
    rank, shard_len = item_factors.shape
    half_blocks = shard_len // TB // 2
    layer = lax.axis_index("layer")
    swap = [(0, 1), (1, 0)]

    with jax.named_scope("gather_items"):
        mine = lax.dynamic_slice_in_dim(item_factors, layer * (shard_len // 2), shard_len // 2, 1)
        mine = mine.reshape(rank, half_blocks, TB).transpose(1, 0, 2)
        own = spread(spread(mine, "item_z"), "item_x")
        own = own.reshape(SIDE * SIDE, half_blocks, rank, TB)
        other = lax.ppermute(own, "layer", swap)

    with jax.named_scope("tiles"):
        keep, send, user_part = tile_terms(
            tile_rows, tile_cols, layer.reshape(1).astype(jnp.int32), user_factors, own, other,
            ratings, masks,
        )

    with jax.named_scope("scatter_items"):
        both = (keep.astype(F32) + lax.ppermute(send, "layer", swap).astype(F32)).astype(BF16)
        both = both.reshape(SIDE, SIDE, half_blocks, rank, TB)
        over_x = lax.all_to_all(both, "item_x", 0, 0)
        over_x = over_x.astype(F32).sum(0).astype(BF16)
        over_item = lax.all_to_all(over_x, "item_z", 0, 0).astype(F32).sum(0)

    with jax.named_scope("sum_users"):
        over_z = spread(over_item.astype(BF16), "user_z").astype(F32).sum(0)
        item_half = spread(over_z, "user_y").sum(0)

    with jax.named_scope("join_layers"):
        joined = jnp.concatenate([item_half, user_part], axis=0)
        joined = lax.all_gather(joined, "layer")
        item_total = joined[:, :half_blocks].reshape(2 * half_blocks, rank, TB)
        user_total = joined[0, half_blocks:] + joined[1, half_blocks:]
        item_total = item_total.transpose(1, 0, 2).reshape(rank, shard_len)
        user_total = user_total.transpose(1, 0, 2).reshape(user_factors.shape)
        grad_users = LOSS_SCALE * user_total + DECAY * user_factors.astype(F32)
        grad_items = LOSS_SCALE * item_total + DECAY * item_factors.astype(F32)
    return (grad_users, grad_items)


def solution(mesh):
    fine = Mesh(
        mesh.devices.reshape(SIDE, SIDE, SIDE, SIDE, 2),
        ("user_y", "user_z", "item_x", "item_z", "layer"),
    )
    users = ("user_y", "user_z")
    items = ("item_x", "item_z")
    everywhere = users + items + ("layer",)
    return jax.shard_map(
        body,
        mesh=fine,
        in_specs=(
            P(None, users + items),
            P(None, items),
            P(everywhere, None, None),
            P(everywhere, None, None),
            P(everywhere),
            P(everywhere),
        ),
        out_specs=(P(None, users + items), P(None, items)),
        check_vma=False,
    )
```

time: 716 us -> 141 us (0.20)
  waiting for transfers between devices: 537 us -> 4.53 us
  blocking collectives: 0 us -> 105 us
  starting transfers between devices: 66.7 us -> 8.33 us
  matrix products: 47.9 us -> 0 us
  local copies, waits for them, and re-layouts: 41.2 us -> 2.67 us
  Pallas kernels: 0 us -> 16.8 us
  between operations: 14.1 us -> 0.8 us
    psum x2 -> x0, waiting for transfers between devices: 388 us -> none  [the longest x1 343 us: body(): item_total = lax.psum(carried, ('user', 'layer'))]
    ppermute x32 -> x2, waiting for transfers between devices: 148 us -> 4.53 us  [the longest x1 2.26 us: body(): other = lax.ppermute(own, 'layer', swap)]
    all_to_all x0 -> x6, blocking collectives: none -> 95.7 us  [the longest x4 68.4 us: spread(): return lax.all_to_all(copies, axis, 0, 0)]
    ppermute x32 -> x2, starting transfers between devices: 66.6 us -> 8.33 us  [the longest x1 6.04 us: body(): other = lax.ppermute(own, 'layer', swap)]
    dot_general x112 -> x0, matrix products: 47.9 us -> none  [the longest x16 20.1 us: shard_terms(): jnp.einsum('bjy,bjf->jyf', user_portion, item_portion, preferred_element_...]
    dynamic_slice x48 -> x1, local copies, waits for them, and re-layouts: 36.9 us -> 0.85 us  [body(): lax.dynamic_slice_in_dim(item_factors, layer * (shard_len // 2), shard_le...]
    pallas_call x0 -> x1, Pallas kernels: none -> 16.8 us  [tile_terms(): pl.pallas_call(tile_kernel, grid_spec=pltpu.PrefetchScalarGridSpec(num_sc...]
    all_gather x0 -> x1, blocking collectives: none -> 9.26 us  [body(): joined = lax.all_gather(joined, 'layer')]
  transfers between devices with their start and end apart: 34 -> 2, of which waited for: 32 -> 2; matrix products, arithmetic and copies ran while one was open for 13% -> 0% of each run, Pallas kernels for 0% -> 0%
where the time goes in v1:
time: 141 us; the launch traced here: 140 us
  blocking collectives  105 us (74%)
  Pallas kernels  16.8 us (12%)
  starting transfers between devices  8.33 us (6%)
  waiting for transfers between devices  4.53 us (3%)
  local copies, waits for them, and re-layouts  2.67 us (2%)
  other arithmetic  2.23 us (2%)
    all_to_all x4, blocking collectives, spread(): return lax.all_to_all(copies, axis, 0, 0)  68.4 us
    all_to_all x1, blocking collectives, body(): over_x = lax.all_to_all(both, 'item_x', 0, 0)  17.3 us
    pallas_call x1, Pallas kernels, tile_terms(): pl.pallas_call(tile_kernel, grid_spec=pltpu.PrefetchScalarGridSpec(num_sc...  16.8 us
    all_to_all x1, blocking collectives, body(): over_item = lax.all_to_all(over_x, 'item_z', 0, 0).astype(F32).sum(0)  10.1 us
    all_gather x1, blocking collectives, body(): joined = lax.all_gather(joined, 'layer')  9.26 us
    ppermute x1, starting transfers between devices, body(): other = lax.ppermute(own, 'layer', swap)  6.04 us
  transfers between devices with their start and end apart: 2, of which 2 were waited for; matrix products, arithmetic and copies ran while one was open for 0% of the time, Pallas kernels for 0%

profile of v1, /device:TPU:1, one launch (start us, length us, event | category | flops | bytes accessed | tf_op | source)
XLA Modules:
  0.0 140.4 jit_solution(8545984648446952115)
XLA Ops:
  0.6 0.8 constant_dynamic-slice_fusion
  1.5 0.0 copy-start
  1.5 0.0 copy-start.2
  1.6 0.0 copy-start.3
  1.6 0.0 copy-start.4
  1.6 12.5 %all_to_all.30 = bf16[4,4,64,128]{3,2,1,0:T(8,128)(2,1)S(1)} all-to-all(bf16[4,4,64,128]{3,2,1,0:T(8,128)(2,1)S(1)} %broadcast_in_dim.8), channel_id=1, replica_groups=mesh['user_y'=4,'user_z'=4,'item_x'=4,'item_z'=4,'layer'=2] {'item_z'}, dimensions={0} | all-to-all | bytes 524288 | tf_op jit(solution)/shard_map/gather_items/all_to_all | solution.py:104
  14.1 0.2 broadcast_in_dim.9
  14.4 16.6 %all_to_all.31 = bf16[4,4,4,64,128]{4,3,2,1,0:T(8,128)(2,1)S(1)} all-to-all(bf16[4,4,4,64,128]{4,3,2,1,0:T(8,128)(2,1)S(1)} %broadcast_in_dim.9), channel_id=1, replica_groups=mesh['user_y'=4,'user_z'=4,'item_x'=4,'item_z'=4,'layer'=2] {'item_x'}, dimensions={0} | all-to-all | bytes 2097152 | tf_op jit(solution)/shard_map/gather_items/all_to_all | solution.py:104
  31.0 6.0 %collective-permute-start = (bf16[16,4,64,128]{3,2,1,0:T(8,128)(2,1)S(1)}, bf16[16,4,64,128]{3,2,1,0:T(8,128)(2,1)S(1)}, u32[]{:S(2)}, u32[]{:S(2)}) collective-permute-start(bf16[16,4,64,128]{3,2,1,0:T(8,128)(2,1)S(1)} %bitcast.18), channel_id=1, source_target_pairs={{0,1},{1,0},{2,3},{3,2},{4,5},{5,4},{6,7},{7,6},{8,9},{9,8},{10,11... | collective-permute-start | bytes 3145736 | tf_op jit(solution)/shard_map/gather_items/ppermute | solution.py:118
  37.0 2.3 %collective-permute-done.other_ref = bf16[16,4,64,128]{3,2,1,0:T(8,128)(2,1)S(1)} collective-permute-done((bf16[16,4,64,128]{3,2,1,0:T(8,128)(2,1)S(1)}, bf16[16,4,64,128]{3,2,1,0:T(8,128)(2,1)S(1)}, u32[]{:S(2)}, u32[]{:S(2)}) %collective-permute-start) | collective-permute-done | bytes 1048608 | tf_op jit(solution)/shard_map/gather_items/ppermute | solution.py:118
  39.3 0.0 copy-done
  39.3 0.0 copy-done.2
  39.3 0.0 copy-done.3
  39.3 0.0 copy-done.4
  39.3 0.0 copy-start.1
  39.3 1.2 copy-done.1
  40.5 16.8 %tile_terms.1 = (bf16[16,4,64,128]{3,2,1,0:T(8,128)(2,1)S(1)}, bf16[16,4,64,128]{3,2,1,0:T(8,128)(2,1)S(1)}, f32[4,64,128]{2,1,0:T(8,128)S(1)}) custom-call(s32[128]{0:T(128)S(1)} %copy-done.3, s32[128]{0:T(128)S(1)} %copy-done.4, s32[1]{0:T(128)} %bitcast.layer_ref, bf16[64,512]{1,0:T(8,128)(2,1)S(1)} %copy-done.2, bf16[16,4,64,128]{3,2,1,0:T(8,128)(2,1)S(1)} %bitcast.19, ...), custom_call_target="tpu_custom_call" | custom-call | tf_op jit(solution)/shard_map/tiles/tile_terms/pallas_call | solution.py:70
  57.4 2.3 %collective-permute-start.1 = (bf16[16,4,64,128]{3,2,1,0:T(8,128)(2,1)S(1)}, bf16[16,4,64,128]{3,2,1,0:T(8,128)(2,1)S(1)}, u32[]{:S(2)}, u32[]{:S(2)}) collective-permute-start(bf16[16,4,64,128]{3,2,1,0:T(8,128)(2,1)S(1)} %get-tuple-element.6), channel_id=1, source_target_pairs={{0,1},{1,0},{2,3},{3,2},{4,5},{5,4},{6,7},{7,6},{8,9},{9,8},{10,11... | collective-permute-start | bytes 3145736 | tf_op jit(solution)/shard_map/scatter_items/ppermute | solution.py:127
  59.7 2.3 %collective-permute-done.1 = bf16[16,4,64,128]{3,2,1,0:T(8,128)(2,1)S(1)} collective-permute-done((bf16[16,4,64,128]{3,2,1,0:T(8,128)(2,1)S(1)}, bf16[16,4,64,128]{3,2,1,0:T(8,128)(2,1)S(1)}, u32[]{:S(2)}, u32[]{:S(2)}) %collective-permute-start.1) | collective-permute-done | bytes 1048608 | tf_op jit(solution)/shard_map/scatter_items/ppermute | solution.py:127
  61.9 0.4 add_convert_fusion
  62.4 17.3 %all_to_all.32 = bf16[4,4,4,64,128]{4,3,2,1,0:T(8,128)(2,1)S(1)} all-to-all(bf16[4,4,4,64,128]{4,3,2,1,0:T(8,128)(2,1)S(1)} %bitcast.20), channel_id=1, replica_groups=mesh['user_y'=4,'user_z'=4,'item_x'=4,'item_z'=4,'layer'=2] {'item_x'}, dimensions={0} | all-to-all | bytes 2097152 | tf_op jit(solution)/shard_map/scatter_items/all_to_all | solution.py:129
  79.7 0.2 reduce_sum.42
  79.9 10.1 %all_to_all.33 = bf16[4,4,64,128]{3,2,1,0:T(8,128)(2,1)S(1)} all-to-all(bf16[4,4,64,128]{3,2,1,0:T(8,128)(2,1)S(1)} %reduce_sum.42), channel_id=1, replica_groups=mesh['user_y'=4,'user_z'=4,'item_x'=4,'item_z'=4,'layer'=2] {'item_z'}, dimensions={0} | all-to-all | bytes 524288 | tf_op jit(solution)/shard_map/scatter_items/all_to_all | solution.py:131
  90.1 28.2 %all_to_all.34 = bf16[4,4,64,128]{3,2,1,0:T(8,128)(2,1)S(1)} all-to-all(bf16[4,4,64,128]{3,2,1,0:T(8,128)(2,1)S(1)} %broadcast_in_dim.10), channel_id=1, replica_groups=mesh['user_y'=4,'user_z'=4,'item_x'=4,'item_z'=4,'layer'=2] {'user_z'}, dimensions={0} | all-to-all | bytes 524288 | tf_op jit(solution)/shard_map/sum_users/all_to_all | solution.py:104
  118.4 0.0 copy-start.5
  118.4 11.1 %all_to_all.35 = f32[4,4,64,128]{3,2,1,0:T(8,128)S(1)} all-to-all(f32[4,4,64,128]{3,2,1,0:T(8,128)S(1)} %broadcast_in_dim.11), channel_id=1, replica_groups=mesh['user_y'=4,'user_z'=4,'item_x'=4,'item_z'=4,'layer'=2] {'user_y'}, dimensions={0} | all-to-all | bytes 1048576 | tf_op jit(solution)/shard_map/sum_users/all_to_all | solution.py:104
  129.5 9.3 %all-gather = f32[16,64,128]{2,1,0:T(8,128)S(1)} all-gather(f32[8,64,128]{2,1,0:T(8,128)S(1)} %pad_maximum_fusion), channel_id=2, replica_groups=mesh['user_y'=4,'user_z'=4,'item_x'=4,'item_z'=4,'layer'=2] {'layer'}, dimensions={0}, use_global_device_ids=true | all-gather | bytes 786432 | tf_op jit(solution)/shard_map/join_layers/all_gather | solution.py:139
  138.8 0.7 bitcast_add_fusion.1
  139.5 0.2 copy.18
  139.6 0.0 copy-done.5
  139.6 0.8 bitcast_add_fusion
  (10 shorter events, 0.3 us)
Async XLA Ops:
  1.5 37.8 %copy-start = (bf16[128,128,128]{2,1,0:T(8,128)(2,1)S(1)}, bf16[128,128,128]{2,1,0:T(8,128)(2,1)}, u32[]{:S(2)}) copy-start(bf16[128,128,128]{2,1,0:T(8,128)(2,1)} %rating_ref.1) | copy-start | bytes 12582916
  1.5 37.8 %copy-start.2 = (bf16[64,512]{1,0:T(8,128)(2,1)S(1)}, bf16[64,512]{1,0:T(8,128)(2,1)}, u32[]{:S(2)}) copy-start(bf16[64,512]{1,0:T(8,128)(2,1)} %user_ref.1) | copy-start | bytes 196612
  1.6 37.8 %copy-start.3 = (s32[128]{0:T(128)S(1)}, s32[128]{0:T(128)}, u32[]{:S(2)}) copy-start(s32[128]{0:T(128)} %rows_ref.1) | copy-start | bytes 1540
  1.6 37.7 %copy-start.4 = (s32[128]{0:T(128)S(1)}, s32[128]{0:T(128)}, u32[]{:S(2)}) copy-start(s32[128]{0:T(128)} %cols_ref.1) | copy-start | bytes 1540
  31.0 8.3 %collective-permute-start = (bf16[16,4,64,128]{3,2,1,0:T(8,128)(2,1)S(1)}, bf16[16,4,64,128]{3,2,1,0:T(8,128)(2,1)S(1)}, u32[]{:S(2)}, u32[]{:S(2)}) collective-permute-start(bf16[16,4,64,128]{3,2,1,0:T(8,128)(2,1)S(1)} %bitcast.18), channel_id=1, source_target_pairs={{0,1},{1,0},{2,3},{3,2},{4,5},{5,4},{6,7},{7,6},{8,9},{9,8},{10,11... | collective-permute-start | bytes 3145736 | tf_op jit(solution)/shard_map/gather_items/ppermute | solution.py:118
  39.3 1.2 copy-start.1
  57.4 4.6 %collective-permute-start.1 = (bf16[16,4,64,128]{3,2,1,0:T(8,128)(2,1)S(1)}, bf16[16,4,64,128]{3,2,1,0:T(8,128)(2,1)S(1)}, u32[]{:S(2)}, u32[]{:S(2)}) collective-permute-start(bf16[16,4,64,128]{3,2,1,0:T(8,128)(2,1)S(1)} %get-tuple-element.6), channel_id=1, source_target_pairs={{0,1},{1,0},{2,3},{3,2},{4,5},{5,4},{6,7},{7,6},{8,9},{9,8},{10,11... | collective-permute-start | bytes 3145736 | tf_op jit(solution)/shard_map/scatter_items/ppermute | solution.py:127
  118.4 21.3 %copy-start.5 = (bf16[64,1024]{1,0:T(8,128)(2,1)S(1)}, bf16[64,1024]{1,0:T(8,128)(2,1)}, u32[]{:S(2)}) copy-start(bf16[64,1024]{1,0:T(8,128)(2,1)} %param.7) | copy-start | bytes 393220

commit v2 on v1

--- a/solution.py
+++ b/solution.py
@@ -131,8 +131,8 @@
         over_item = lax.all_to_all(over_x, "item_z", 0, 0).astype(F32).sum(0)
 
     with jax.named_scope("sum_users"):
-        over_z = spread(over_item.astype(BF16), "user_z").astype(F32).sum(0)
-        item_half = spread(over_z, "user_y").sum(0)
+        over_z = lax.all_gather(over_item.astype(BF16), "user_z").astype(F32).sum(0)
+        item_half = lax.all_gather(over_z, "user_y").sum(0)
 
     with jax.named_scope("join_layers"):
         joined = jnp.concatenate([item_half, user_part], axis=0)

time: 141 us -> 136 us (0.965)
  blocking collectives: 105 us -> 101 us
    all_to_all x4 -> x2, blocking collectives: 68.4 us -> 29.1 us  [spread(): return lax.all_to_all(copies, axis, 0, 0)]
    all_gather x0 -> x2, blocking collectives: none -> 33 us  [the longest x1 22.2 us: body(): over_z = lax.all_gather(over_item.astype(BF16), 'user_z').astype(F32).sum(0)]
    all_gather x1, blocking collectives: 9.26 us -> 11.2 us  [body(): joined = lax.all_gather(joined, 'layer')]
where the time goes in v2:
time: 136 us
  blocking collectives  101 us (74%)
  Pallas kernels  16.8 us (12%)
  starting transfers between devices  8.33 us (6%)
  waiting for transfers between devices  4.53 us (3%)
  local copies, waits for them, and re-layouts  2.58 us (2%)
  other arithmetic  2.23 us (2%)
    all_to_all x2, blocking collectives, spread(): return lax.all_to_all(copies, axis, 0, 0)  29.1 us
    all_gather x1, blocking collectives, body(): over_z = lax.all_gather(over_item.astype(BF16), 'user_z').astype(F32).sum(0)  22.2 us
    all_to_all x1, blocking collectives, body(): over_x = lax.all_to_all(both, 'item_x', 0, 0)  17.3 us
    pallas_call x1, Pallas kernels, tile_terms(): pl.pallas_call(tile_kernel, grid_spec=pltpu.PrefetchScalarGridSpec(num_sc...  16.8 us
    all_gather x1, blocking collectives, body(): joined = lax.all_gather(joined, 'layer')  11.2 us
    all_gather x1, blocking collectives, body(): item_half = lax.all_gather(over_z, 'user_y').sum(0)  10.8 us
    all_to_all x1, blocking collectives, body(): over_item = lax.all_to_all(over_x, 'item_z', 0, 0).astype(F32).sum(0)  10.1 us
    ppermute x1, starting transfers between devices, body(): other = lax.ppermute(own, 'layer', swap)  6.04 us
  transfers between devices with their start and end apart: 2, of which 2 were waited for; matrix products, arithmetic and copies ran while one was open for 0% of the time, Pallas kernels for 0%

profile of v2, /device:TPU:1, one launch (start us, length us, event | category | flops | bytes accessed | tf_op | source)
XLA Modules:
  0.0 136.1 jit_solution(17040522658287167518)
XLA Ops:
  0.6 0.8 constant_dynamic-slice_fusion
  1.5 0.0 copy-start
  1.5 0.0 copy-start.2
  1.6 0.0 copy-start.3
  1.6 0.0 copy-start.4
  1.6 12.5 %all_to_all.20 = bf16[4,4,64,128]{3,2,1,0:T(8,128)(2,1)S(1)} all-to-all(bf16[4,4,64,128]{3,2,1,0:T(8,128)(2,1)S(1)} %broadcast_in_dim.4), channel_id=1, replica_groups=mesh['user_y'=4,'user_z'=4,'item_x'=4,'item_z'=4,'layer'=2] {'item_z'}, dimensions={0} | all-to-all | bytes 524288 | tf_op jit(solution)/shard_map/gather_items/all_to_all | solution.py:104
  14.1 0.2 broadcast_in_dim.5
  14.4 16.6 %all_to_all.21 = bf16[4,4,4,64,128]{4,3,2,1,0:T(8,128)(2,1)S(1)} all-to-all(bf16[4,4,4,64,128]{4,3,2,1,0:T(8,128)(2,1)S(1)} %broadcast_in_dim.5), channel_id=1, replica_groups=mesh['user_y'=4,'user_z'=4,'item_x'=4,'item_z'=4,'layer'=2] {'item_x'}, dimensions={0} | all-to-all | bytes 2097152 | tf_op jit(solution)/shard_map/gather_items/all_to_all | solution.py:104
  31.0 6.0 %collective-permute-start = (bf16[16,4,64,128]{3,2,1,0:T(8,128)(2,1)S(1)}, bf16[16,4,64,128]{3,2,1,0:T(8,128)(2,1)S(1)}, u32[]{:S(2)}, u32[]{:S(2)}) collective-permute-start(bf16[16,4,64,128]{3,2,1,0:T(8,128)(2,1)S(1)} %bitcast.21), channel_id=1, source_target_pairs={{0,1},{1,0},{2,3},{3,2},{4,5},{5,4},{6,7},{7,6},{8,9},{9,8},{10,11... | collective-permute-start | bytes 3145736 | tf_op jit(solution)/shard_map/gather_items/ppermute | solution.py:118
  37.0 2.3 %collective-permute-done.other_ref = bf16[16,4,64,128]{3,2,1,0:T(8,128)(2,1)S(1)} collective-permute-done((bf16[16,4,64,128]{3,2,1,0:T(8,128)(2,1)S(1)}, bf16[16,4,64,128]{3,2,1,0:T(8,128)(2,1)S(1)}, u32[]{:S(2)}, u32[]{:S(2)}) %collective-permute-start) | collective-permute-done | bytes 1048608 | tf_op jit(solution)/shard_map/gather_items/ppermute | solution.py:118
  39.3 0.0 copy-done
  39.3 0.0 copy-done.2
  39.3 0.0 copy-done.3
  39.3 0.0 copy-done.4
  39.3 0.0 copy-start.1
  39.3 1.2 copy-done.1
  40.5 16.8 %tile_terms.1 = (bf16[16,4,64,128]{3,2,1,0:T(8,128)(2,1)S(1)}, bf16[16,4,64,128]{3,2,1,0:T(8,128)(2,1)S(1)}, f32[4,64,128]{2,1,0:T(8,128)S(1)}) custom-call(s32[128]{0:T(128)S(1)} %copy-done.3, s32[128]{0:T(128)S(1)} %copy-done.4, s32[1]{0:T(128)} %bitcast.layer_ref, bf16[64,512]{1,0:T(8,128)(2,1)S(1)} %copy-done.2, bf16[16,4,64,128]{3,2,1,0:T(8,128)(2,1)S(1)} %bitcast.22, ...), custom_call_target="tpu_custom_call" | custom-call | tf_op jit(solution)/shard_map/tiles/tile_terms/pallas_call | solution.py:70
  57.4 2.3 %collective-permute-start.1 = (bf16[16,4,64,128]{3,2,1,0:T(8,128)(2,1)S(1)}, bf16[16,4,64,128]{3,2,1,0:T(8,128)(2,1)S(1)}, u32[]{:S(2)}, u32[]{:S(2)}) collective-permute-start(bf16[16,4,64,128]{3,2,1,0:T(8,128)(2,1)S(1)} %get-tuple-element.6), channel_id=1, source_target_pairs={{0,1},{1,0},{2,3},{3,2},{4,5},{5,4},{6,7},{7,6},{8,9},{9,8},{10,11... | collective-permute-start | bytes 3145736 | tf_op jit(solution)/shard_map/scatter_items/ppermute | solution.py:127
  59.7 2.3 %collective-permute-done.1 = bf16[16,4,64,128]{3,2,1,0:T(8,128)(2,1)S(1)} collective-permute-done((bf16[16,4,64,128]{3,2,1,0:T(8,128)(2,1)S(1)}, bf16[16,4,64,128]{3,2,1,0:T(8,128)(2,1)S(1)}, u32[]{:S(2)}, u32[]{:S(2)}) %collective-permute-start.1) | collective-permute-done | bytes 1048608 | tf_op jit(solution)/shard_map/scatter_items/ppermute | solution.py:127
  61.9 0.4 add_convert_fusion
  62.4 17.3 %all_to_all.22 = bf16[4,4,4,64,128]{4,3,2,1,0:T(8,128)(2,1)S(1)} all-to-all(bf16[4,4,4,64,128]{4,3,2,1,0:T(8,128)(2,1)S(1)} %bitcast.23), channel_id=1, replica_groups=mesh['user_y'=4,'user_z'=4,'item_x'=4,'item_z'=4,'layer'=2] {'item_x'}, dimensions={0} | all-to-all | bytes 2097152 | tf_op jit(solution)/shard_map/scatter_items/all_to_all | solution.py:129
  79.7 0.2 reduce_sum.42
  79.9 10.1 %all_to_all.23 = bf16[4,4,64,128]{3,2,1,0:T(8,128)(2,1)S(1)} all-to-all(bf16[4,4,64,128]{3,2,1,0:T(8,128)(2,1)S(1)} %reduce_sum.42), channel_id=1, replica_groups=mesh['user_y'=4,'user_z'=4,'item_x'=4,'item_z'=4,'layer'=2] {'item_z'}, dimensions={0} | all-to-all | bytes 524288 | tf_op jit(solution)/shard_map/scatter_items/all_to_all | solution.py:131
  90.0 22.2 %all-gather = bf16[16,64,128]{2,1,0:T(8,128)(2,1)S(1)} all-gather(bf16[4,64,128]{2,1,0:T(8,128)(2,1)S(1)} %reduce_sum.43), channel_id=2, replica_groups=mesh['user_y'=4,'user_z'=4,'item_x'=4,'item_z'=4,'layer'=2] {'user_z'}, dimensions={0}, use_global_device_ids=true | all-gather | bytes 327680 | tf_op jit(solution)/shard_map/sum_users/all_gather | solution.py:134
  112.3 0.0 copy-start.5
  112.3 10.8 %all-gather.1 = f32[16,64,128]{2,1,0:T(8,128)S(1)} all-gather(f32[4,64,128]{2,1,0:T(8,128)S(1)} %convert_reduce_fusion), channel_id=3, replica_groups=mesh['user_y'=4,'user_z'=4,'item_x'=4,'item_z'=4,'layer'=2] {'user_y'}, dimensions={0}, use_global_device_ids=true | all-gather | bytes 655360 | tf_op jit(solution)/shard_map/sum_users/all_gather | solution.py:135
  123.2 11.2 %all-gather.2 = f32[16,64,128]{2,1,0:T(8,128)S(1)} all-gather(f32[8,64,128]{2,1,0:T(8,128)S(1)} %pad_maximum_fusion), channel_id=4, replica_groups=mesh['user_y'=4,'user_z'=4,'item_x'=4,'item_z'=4,'layer'=2] {'layer'}, dimensions={0}, use_global_device_ids=true | all-gather | bytes 786432 | tf_op jit(solution)/shard_map/join_layers/all_gather | solution.py:139
  134.4 0.7 bitcast_add_fusion.1
  135.1 0.2 copy.18
  135.3 0.0 copy-done.5
  135.3 0.8 bitcast_add_fusion
  (8 shorter events, 0.2 us)
Async XLA Ops:
  1.5 37.8 %copy-start = (bf16[128,128,128]{2,1,0:T(8,128)(2,1)S(1)}, bf16[128,128,128]{2,1,0:T(8,128)(2,1)}, u32[]{:S(2)}) copy-start(bf16[128,128,128]{2,1,0:T(8,128)(2,1)} %rating_ref.1) | copy-start | bytes 12582916
  1.5 37.8 %copy-start.2 = (bf16[64,512]{1,0:T(8,128)(2,1)S(1)}, bf16[64,512]{1,0:T(8,128)(2,1)}, u32[]{:S(2)}) copy-start(bf16[64,512]{1,0:T(8,128)(2,1)} %user_ref.1) | copy-start | bytes 196612
  1.6 37.8 %copy-start.3 = (s32[128]{0:T(128)S(1)}, s32[128]{0:T(128)}, u32[]{:S(2)}) copy-start(s32[128]{0:T(128)} %rows_ref.1) | copy-start | bytes 1540
  1.6 37.7 %copy-start.4 = (s32[128]{0:T(128)S(1)}, s32[128]{0:T(128)}, u32[]{:S(2)}) copy-start(s32[128]{0:T(128)} %cols_ref.1) | copy-start | bytes 1540
  31.0 8.3 %collective-permute-start = (bf16[16,4,64,128]{3,2,1,0:T(8,128)(2,1)S(1)}, bf16[16,4,64,128]{3,2,1,0:T(8,128)(2,1)S(1)}, u32[]{:S(2)}, u32[]{:S(2)}) collective-permute-start(bf16[16,4,64,128]{3,2,1,0:T(8,128)(2,1)S(1)} %bitcast.21), channel_id=1, source_target_pairs={{0,1},{1,0},{2,3},{3,2},{4,5},{5,4},{6,7},{7,6},{8,9},{9,8},{10,11... | collective-permute-start | bytes 3145736 | tf_op jit(solution)/shard_map/gather_items/ppermute | solution.py:118
  39.3 1.2 copy-start.1
  57.4 4.6 %collective-permute-start.1 = (bf16[16,4,64,128]{3,2,1,0:T(8,128)(2,1)S(1)}, bf16[16,4,64,128]{3,2,1,0:T(8,128)(2,1)S(1)}, u32[]{:S(2)}, u32[]{:S(2)}) collective-permute-start(bf16[16,4,64,128]{3,2,1,0:T(8,128)(2,1)S(1)} %get-tuple-element.6), channel_id=1, source_target_pairs={{0,1},{1,0},{2,3},{3,2},{4,5},{5,4},{6,7},{7,6},{8,9},{9,8},{10,11... | collective-permute-start | bytes 3145736 | tf_op jit(solution)/shard_map/scatter_items/ppermute | solution.py:127
  112.3 23.0 %copy-start.5 = (bf16[64,1024]{1,0:T(8,128)(2,1)S(1)}, bf16[64,1024]{1,0:T(8,128)(2,1)}, u32[]{:S(2)}) copy-start(bf16[64,1024]{1,0:T(8,128)(2,1)} %param.7) | copy-start | bytes 393220

commit v3 on v2

v3 whole, which is shorter than its diff:
```python
import jax
import jax.numpy as jnp
from jax import lax
from jax.experimental import pallas as pl
from jax.experimental.pallas import tpu as pltpu
from jax.sharding import Mesh
from jax.sharding import PartitionSpec as P

LOSS_SCALE = 0.0625
DECAY = 0.1
TB = 128
SIDE = 4
BF16 = jnp.bfloat16
F32 = jnp.float32


def tile_kernel(
    rows_ref, cols_ref, layer_ref, user_ref, own_ref, other_ref, rating_ref, mask_ref,
    keep_ref, send_ref, user_out_ref, user_t_ref, user_acc_ref, item_acc_ref, residual_ref,
):
    step = pl.program_id(0)
    layer = layer_ref[0]
    tiles = rating_ref.shape[0]
    shards, half_blocks = own_ref.shape[:2]
    per_shard = tiles // shards
    user_blocks = user_out_ref.shape[0]
    words = mask_ref.shape[1]

    @pl.when(step == 0)
    def _():
        user_acc_ref[...] = jnp.zeros_like(user_acc_ref)
        for b in range(user_blocks):
            block = user_ref[:, b * TB:(b + 1) * TB].astype(F32)
            user_t_ref[b] = block.T.astype(BF16)

    item_acc_ref[...] = jnp.zeros_like(item_acc_ref)

    def place(t):
        return rows_ref[step * tiles + t], cols_ref[step * tiles + t]

    def item_of(t, c):
        at = c % half_blocks
        mine, theirs = own_ref[t // per_shard, at], other_ref[t // per_shard, at]
        return jnp.where(c // half_blocks == layer, mine, theirs)

    bit = jnp.left_shift(jnp.int32(1), lax.broadcasted_iota(jnp.int32, (8, TB), 0))
    for t in range(tiles):
        b, c = place(t)
        scores = jnp.dot(user_t_ref[b], item_of(t, c), preferred_element_type=F32)
        difference = scores - rating_ref[t].astype(F32)
        parts = []
        for w in range(words):
            word = jnp.broadcast_to(mask_ref[t, w:w + 1, :], (8, TB))
            parts.append(jnp.where((word & bit) != 0, difference[w * 8:(w + 1) * 8], 0.0))
        residual_ref[t] = jnp.concatenate(parts, axis=0).astype(BF16)

    for t in range(tiles):
        b, c = place(t)
        residual = residual_ref[t]
        user = user_ref[:, pl.ds(pl.multiple_of(b * TB, TB), TB)]
        item_acc_ref[(t // per_shard) * 2 * half_blocks + c] += jnp.dot(
            user, residual, preferred_element_type=F32
        )
        user_acc_ref[b] += lax.dot_general(
            residual, item_of(t, c), (((1,), (1,)), ((), ())), preferred_element_type=F32
        )

    for g in range(shards):
        for j in range(half_blocks):
            at = g * 2 * half_blocks + j
            keep_ref[g, j] = item_acc_ref[at + layer * half_blocks].astype(BF16)
            send_ref[g, j] = item_acc_ref[at + (1 - layer) * half_blocks].astype(BF16)

    @pl.when(step == pl.num_programs(0) - 1)
    def _():
        for b in range(user_blocks):
            user_out_ref[b] = user_acc_ref[b].T


def tile_terms(rows, cols, layer, user_factors, own, other, ratings, masks):
    shards, half_blocks, rank, _ = own.shape
    tiles = ratings.shape[0] // shards * SIDE
    user_blocks = user_factors.shape[1] // TB
    words = masks.shape[1]
    half = pl.BlockSpec((SIDE, half_blocks, rank, TB), lambda i, *_: (i, 0, 0, 0))
    return pl.pallas_call(
        tile_kernel,
        grid_spec=pltpu.PrefetchScalarGridSpec(
            num_scalar_prefetch=3,
            grid=(shards // SIDE,),
            in_specs=[
                pl.BlockSpec(user_factors.shape, lambda i, *_: (0, 0)),
                half,
                half,
                pl.BlockSpec((tiles, TB, TB), lambda i, *_: (i, 0, 0)),
                pl.BlockSpec((tiles, words, TB), lambda i, *_: (i, 0, 0)),
            ],
            out_specs=[
                half,
                half,
                pl.BlockSpec((user_blocks, rank, TB), lambda i, *_: (0, 0, 0)),
            ],
            scratch_shapes=[
                pltpu.VMEM((user_blocks, TB, rank), BF16),
                pltpu.VMEM((user_blocks, TB, rank), F32),
                pltpu.VMEM((SIDE * 2 * half_blocks, rank, TB), F32),
                pltpu.VMEM((tiles, TB, TB), BF16),
            ],
        ),
        out_shape=[
            jax.ShapeDtypeStruct(own.shape, BF16),
            jax.ShapeDtypeStruct(own.shape, BF16),
            jax.ShapeDtypeStruct((user_blocks, rank, TB), F32),
        ],
        compiler_params=pltpu.CompilerParams(vmem_limit_bytes=32 * 1024 * 1024),
        name="tile_terms",
    )(rows, cols, layer, user_factors, own, other, ratings, masks)


def spread(block, axes):
    copies = jnp.broadcast_to(block[None], (lax.axis_size(axes),) + block.shape)
    return lax.all_to_all(copies, axes, 0, 0)


def body(user_factors, item_factors, ratings, masks, tile_rows, tile_cols):
    rank, shard_len = item_factors.shape
    half_blocks = shard_len // TB // 2
    layer = lax.axis_index("layer")
    swap = [(0, 1), (1, 0)]

    with jax.named_scope("gather_items"):
        mine = lax.dynamic_slice_in_dim(
            item_factors.reshape(rank, 2 * half_blocks, TB), layer * half_blocks, half_blocks, 1
        )
        own = spread(spread(mine.transpose(1, 0, 2), "item_z"), "item_x")
        own = own.reshape(SIDE * SIDE, half_blocks, rank, TB)
        other = lax.ppermute(own, "layer", swap)

    with jax.named_scope("tiles"):
        keep, send, user_part = tile_terms(
            tile_rows, tile_cols, layer.reshape(1).astype(jnp.int32), user_factors, own, other,
            ratings, masks,
        )

    with jax.named_scope("scatter_items"):
        both = (keep.astype(F32) + lax.ppermute(send, "layer", swap).astype(F32)).astype(BF16)
        both = both.reshape(SIDE, SIDE, half_blocks, rank, TB).transpose(2, 0, 1, 3, 4)
        both = both.reshape(half_blocks * SIDE, SIDE, rank, TB)
        part = lax.all_to_all(both, ("user_y", "item_x"), 0, 0)
        part = part.astype(F32).sum(0).astype(BF16)

    with jax.named_scope("sum_along_z"):
        copies = jnp.broadcast_to(part[None], (SIDE,) + part.shape)
        copies = copies.reshape((SIDE * SIDE,) + part.shape[1:])
        part = lax.all_to_all(copies, ("user_z", "item_z"), 0, 0).astype(F32).sum(0)

    with jax.named_scope("join"):
        item_half = spread(part, "user_y")
        joined = lax.all_gather(jnp.concatenate([item_half, user_part], axis=0), "layer")
        item_total = joined[:, :half_blocks].reshape(2 * half_blocks, rank, TB)
        user_total = joined[0, half_blocks:] + joined[1, half_blocks:]
        item_total = item_total.transpose(1, 0, 2).reshape(rank, shard_len)
        user_total = user_total.transpose(1, 0, 2).reshape(user_factors.shape)
        grad_users = LOSS_SCALE * user_total + DECAY * user_factors.astype(F32)
        grad_items = LOSS_SCALE * item_total + DECAY * item_factors.astype(F32)
    return (grad_users, grad_items)


def solution(mesh):
    fine = Mesh(
        mesh.devices.reshape(SIDE, SIDE, SIDE, SIDE, 2),
        ("user_y", "user_z", "item_x", "item_z", "layer"),
    )
    users = ("user_y", "user_z")
    items = ("item_x", "item_z")
    everywhere = users + items + ("layer",)
    return jax.shard_map(
        body,
        mesh=fine,
        in_specs=(
            P(None, users + items),
            P(None, items),
            P(everywhere, None, None),
            P(everywhere, None, None),
            P(everywhere),
            P(everywhere),
        ),
        out_specs=(P(None, users + items), P(None, items)),
        check_vma=False,
    )
```

time: 136 us -> 117 us (0.86)
  Pallas kernels: 16.8 us -> 6.3 us
  blocking collectives: 101 us -> 92.1 us
    all_gather x3 -> x1, blocking collectives: 44.3 us -> 9.78 us  [body(): lax.all_gather(jnp.concatenate([item_half, user_part], axis=0), 'layer')]
    all_to_all x4 -> x5, blocking collectives: 56.5 us -> 82.3 us  [the longest x3 36.3 us: spread(): return lax.all_to_all(copies, axes, 0, 0)]
    pallas_call x1, Pallas kernels: 16.8 us -> 6.3 us  [tile_terms(): pl.pallas_call(tile_kernel, grid_spec=pltpu.PrefetchScalarGridSpec(num_sc...]
where the time goes in v3:
time: 117 us
  blocking collectives  92.1 us (79%)
  starting transfers between devices  8.33 us (7%)
  Pallas kernels  6.3 us (5%)
  waiting for transfers between devices  4.53 us (4%)
  local copies, waits for them, and re-layouts  2.82 us (2%)
  other arithmetic  2.16 us (2%)
    all_to_all x3, blocking collectives, spread(): return lax.all_to_all(copies, axes, 0, 0)  36.3 us
    all_to_all x1, blocking collectives, body(): part = lax.all_to_all(copies, ('user_z', 'item_z'), 0, 0).astype(F32).sum(0)  24.9 us
    all_to_all x1, blocking collectives, body(): part = lax.all_to_all(both, ('user_y', 'item_x'), 0, 0)  21 us
    all_gather x1, blocking collectives, body(): lax.all_gather(jnp.concatenate([item_half, user_part], axis=0), 'layer')  9.78 us
    pallas_call x1, Pallas kernels, tile_terms(): pl.pallas_call(tile_kernel, grid_spec=pltpu.PrefetchScalarGridSpec(num_sc...  6.3 us
    ppermute x1, starting transfers between devices, body(): other = lax.ppermute(own, 'layer', swap)  6.04 us
  transfers between devices with their start and end apart: 2, of which 2 were waited for; matrix products, arithmetic and copies ran while one was open for 0% of the time, Pallas kernels for 0%

profile of v3, /device:TPU:1, one launch (start us, length us, event | category | flops | bytes accessed | tf_op | source)
XLA Modules:
  0.0 117.0 jit_solution(9879836351487872084)
XLA Ops:
  0.6 0.9 copy.24
  1.6 0.0 copy-start
  1.6 0.0 copy-start.2
  1.7 0.0 copy-start.3
  1.7 0.0 copy-start.4
  1.7 12.5 %all_to_all.25 = bf16[4,4,64,128]{3,2,1,0:T(8,128)(2,1)S(1)} all-to-all(bf16[4,4,64,128]{3,2,1,0:T(8,128)(2,1)S(1)} %broadcast_in_dim.8), channel_id=1, replica_groups=mesh['user_y'=4,'user_z'=4,'item_x'=4,'item_z'=4,'layer'=2] {'item_z'}, dimensions={0} | all-to-all | bytes 524288 | tf_op jit(solution)/shard_map/gather_items/all_to_all | solution.py:122
  14.2 0.2 broadcast_in_dim.9
  14.5 16.6 %all_to_all.26 = bf16[4,4,4,64,128]{4,3,2,1,0:T(8,128)(2,1)S(1)} all-to-all(bf16[4,4,4,64,128]{4,3,2,1,0:T(8,128)(2,1)S(1)} %broadcast_in_dim.9), channel_id=1, replica_groups=mesh['user_y'=4,'user_z'=4,'item_x'=4,'item_z'=4,'layer'=2] {'item_x'}, dimensions={0} | all-to-all | bytes 2097152 | tf_op jit(solution)/shard_map/gather_items/all_to_all | solution.py:122
  31.1 6.0 %collective-permute-start = (bf16[16,4,64,128]{3,2,1,0:T(8,128)(2,1)S(1)}, bf16[16,4,64,128]{3,2,1,0:T(8,128)(2,1)S(1)}, u32[]{:S(2)}, u32[]{:S(2)}) collective-permute-start(bf16[16,4,64,128]{3,2,1,0:T(8,128)(2,1)S(1)} %bitcast.25), channel_id=1, source_target_pairs={{0,1},{1,0},{2,3},{3,2},{4,5},{5,4},{6,7},{7,6},{8,9},{9,8},{10,11... | collective-permute-start | bytes 3145736 | tf_op jit(solution)/shard_map/gather_items/ppermute | solution.py:137
  37.1 2.3 %collective-permute-done.other_ref = bf16[16,4,64,128]{3,2,1,0:T(8,128)(2,1)S(1)} collective-permute-done((bf16[16,4,64,128]{3,2,1,0:T(8,128)(2,1)S(1)}, bf16[16,4,64,128]{3,2,1,0:T(8,128)(2,1)S(1)}, u32[]{:S(2)}, u32[]{:S(2)}) %collective-permute-start) | collective-permute-done | bytes 1048608 | tf_op jit(solution)/shard_map/gather_items/ppermute | solution.py:137
  39.4 0.0 copy-done
  39.4 0.0 copy-done.2
  39.4 0.0 copy-done.3
  39.4 0.0 copy-done.4
  39.4 0.0 copy-start.1
  39.4 1.2 %copy-done.1 = s32[128,16,128]{2,1,0:T(8,128)S(1)} copy-done((s32[128,16,128]{2,1,0:T(8,128)S(1)}, s32[128,16,128]{2,1,0:T(8,128)}, u32[]{:S(2)}) %copy-start.1) | copy-done | bytes 1048600
  40.6 6.3 %tile_terms.1 = (bf16[16,4,64,128]{3,2,1,0:T(8,128)(2,1)S(1)}, bf16[16,4,64,128]{3,2,1,0:T(8,128)(2,1)S(1)}, f32[4,64,128]{2,1,0:T(8,128)S(1)}) custom-call(s32[128]{0:T(128)S(1)} %copy-done.3, s32[128]{0:T(128)S(1)} %copy-done.4, s32[1]{0:T(128)} %bitcast.layer_ref, bf16[64,512]{1,0:T(8,128)(2,1)S(1)} %copy-done.2, bf16[16,4,64,128]{3,2,1,0:T(8,128)(2,1)S(1)} %bitcast.26, ...), custom_call_target="tpu_custom_call" | custom-call | tf_op jit(solution)/shard_map/tiles/tile_terms/pallas_call | solution.py:86
  47.0 2.3 %collective-permute-start.1 = (bf16[16,4,64,128]{3,2,1,0:T(8,128)(2,1)S(1)}, bf16[16,4,64,128]{3,2,1,0:T(8,128)(2,1)S(1)}, u32[]{:S(2)}, u32[]{:S(2)}) collective-permute-start(bf16[16,4,64,128]{3,2,1,0:T(8,128)(2,1)S(1)} %get-tuple-element.6), channel_id=1, source_target_pairs={{0,1},{1,0},{2,3},{3,2},{4,5},{5,4},{6,7},{7,6},{8,9},{9,8},{10,11... | collective-permute-start | bytes 3145736 | tf_op jit(solution)/shard_map/scatter_items/ppermute | solution.py:146
  49.2 2.3 %collective-permute-done.1 = bf16[16,4,64,128]{3,2,1,0:T(8,128)(2,1)S(1)} collective-permute-done((bf16[16,4,64,128]{3,2,1,0:T(8,128)(2,1)S(1)}, bf16[16,4,64,128]{3,2,1,0:T(8,128)(2,1)S(1)}, u32[]{:S(2)}, u32[]{:S(2)}) %collective-permute-start.1) | collective-permute-done | bytes 1048608 | tf_op jit(solution)/shard_map/scatter_items/ppermute | solution.py:146
  51.5 0.4 add_convert_fusion
  52.0 0.1 copy.20
  52.0 21.0 %all_to_all.27 = bf16[16,4,64,128]{3,2,1,0:T(8,128)(2,1)S(1)} all-to-all(bf16[16,4,64,128]{3,2,1,0:T(8,128)(2,1)S(1)} %bitcast.28), channel_id=1, replica_groups=mesh['user_y'=4,'user_z'=4,'item_x'=4,'item_z'=4,'layer'=2] {'user_y','i..., dimensions={0} | all-to-all | bytes 2097152 | tf_op jit(solution)/shard_map/scatter_items/all_to_all | solution.py:149
  73.1 0.2 reduce_sum.21
  73.3 0.0 copy-start.5
  73.3 24.9 %all_to_all.28 = bf16[16,64,128]{2,1,0:T(8,128)(2,1)S(1)} all-to-all(bf16[16,64,128]{2,1,0:T(8,128)(2,1)S(1)} %bitcast.31), channel_id=1, replica_groups=mesh['user_y'=4,'user_z'=4,'item_x'=4,'item_z'=4,'layer'=2] {'user_z','i..., dimensions={0} | all-to-all | bytes 524288 | tf_op jit(solution)/shard_map/sum_along_z/all_to_all | solution.py:155
  98.3 7.2 %all_to_all.29 = f32[4,64,128]{2,1,0:T(8,128)S(1)} all-to-all(f32[4,64,128]{2,1,0:T(8,128)S(1)} %broadcast_in_dim.11), channel_id=1, replica_groups=mesh['user_y'=4,'user_z'=4,'item_x'=4,'item_z'=4,'layer'=2] {'user_y'}, dimensions={0} | all-to-all | bytes 262144 | tf_op jit(solution)/shard_map/join/all_to_all | solution.py:122
  105.6 9.8 %all-gather = f32[16,64,128]{2,1,0:T(8,128)S(1)} all-gather(f32[8,64,128]{2,1,0:T(8,128)S(1)} %pad_maximum_fusion), channel_id=2, replica_groups=mesh['user_y'=4,'user_z'=4,'item_x'=4,'item_z'=4,'layer'=2] {'layer'}, dimensions={0}, use_global_device_ids=true | all-gather | bytes 786432 | tf_op jit(solution)/shard_map/join/all_gather | solution.py:159
  115.3 0.7 bitcast_add_fusion.1
  116.0 0.2 copy.22
  116.2 0.0 copy-done.5
  116.2 0.8 bitcast_add_fusion
  (8 shorter events, 0.2 us)
Async XLA Ops:
  1.6 37.8 %copy-start = (bf16[128,128,128]{2,1,0:T(8,128)(2,1)S(1)}, bf16[128,128,128]{2,1,0:T(8,128)(2,1)}, u32[]{:S(2)}) copy-start(bf16[128,128,128]{2,1,0:T(8,128)(2,1)} %rating_ref.1) | copy-start | bytes 12582916
  1.6 37.8 %copy-start.2 = (bf16[64,512]{1,0:T(8,128)(2,1)S(1)}, bf16[64,512]{1,0:T(8,128)(2,1)}, u32[]{:S(2)}) copy-start(bf16[64,512]{1,0:T(8,128)(2,1)} %user_ref.1) | copy-start | bytes 196612
  1.7 37.8 %copy-start.3 = (s32[128]{0:T(128)S(1)}, s32[128]{0:T(128)}, u32[]{:S(2)}) copy-start(s32[128]{0:T(128)} %rows_ref.1) | copy-start | bytes 1540
  1.7 37.7 %copy-start.4 = (s32[128]{0:T(128)S(1)}, s32[128]{0:T(128)}, u32[]{:S(2)}) copy-start(s32[128]{0:T(128)} %cols_ref.1) | copy-start | bytes 1540
  31.1 8.3 %collective-permute-start = (bf16[16,4,64,128]{3,2,1,0:T(8,128)(2,1)S(1)}, bf16[16,4,64,128]{3,2,1,0:T(8,128)(2,1)S(1)}, u32[]{:S(2)}, u32[]{:S(2)}) collective-permute-start(bf16[16,4,64,128]{3,2,1,0:T(8,128)(2,1)S(1)} %bitcast.25), channel_id=1, source_target_pairs={{0,1},{1,0},{2,3},{3,2},{4,5},{5,4},{6,7},{7,6},{8,9},{9,8},{10,11... | collective-permute-start | bytes 3145736 | tf_op jit(solution)/shard_map/gather_items/ppermute | solution.py:137
  39.4 1.2 %copy-start.1 = (s32[128,16,128]{2,1,0:T(8,128)S(1)}, s32[128,16,128]{2,1,0:T(8,128)}, u32[]{:S(2)}) copy-start(s32[128,16,128]{2,1,0:T(8,128)} %mask_ref.1) | copy-start | bytes 3145732
  47.0 4.6 %collective-permute-start.1 = (bf16[16,4,64,128]{3,2,1,0:T(8,128)(2,1)S(1)}, bf16[16,4,64,128]{3,2,1,0:T(8,128)(2,1)S(1)}, u32[]{:S(2)}, u32[]{:S(2)}) collective-permute-start(bf16[16,4,64,128]{3,2,1,0:T(8,128)(2,1)S(1)} %get-tuple-element.6), channel_id=1, source_target_pairs={{0,1},{1,0},{2,3},{3,2},{4,5},{5,4},{6,7},{7,6},{8,9},{9,8},{10,11... | collective-permute-start | bytes 3145736 | tf_op jit(solution)/shard_map/scatter_items/ppermute | solution.py:146
  73.3 42.9 %copy-start.5 = (bf16[64,1024]{1,0:T(8,128)(2,1)S(1)}, bf16[64,1024]{1,0:T(8,128)(2,1)}, u32[]{:S(2)}) copy-start(bf16[64,1024]{1,0:T(8,128)(2,1)} %param.7) | copy-start | bytes 393220

commit v4 on v3

v4 whole, which is shorter than its diff:
```python
import jax
import jax.numpy as jnp
from jax import lax
from jax.experimental import pallas as pl
from jax.experimental.pallas import tpu as pltpu
from jax.sharding import Mesh
from jax.sharding import PartitionSpec as P

LOSS_SCALE = 0.0625
DECAY = 0.1
TB = 128
SIDE = 4
BF16 = jnp.bfloat16
F32 = jnp.float32


def tile_place(rows_ref, cols_ref, t, tiles):
    at = pl.program_id(0) * tiles + t
    return rows_ref[at], cols_ref[at]


def item_block(own_ref, other_ref, layer, shard, c):
    half_blocks = own_ref.shape[1]
    at = c % half_blocks
    return jnp.where(c // half_blocks == layer, own_ref[shard, at], other_ref[shard, at])


def item_kernel(
    rows_ref, cols_ref, layer_ref, user_ref, own_ref, other_ref, rating_ref, mask_ref,
    keep_ref, send_ref, residual_ref, user_t_ref, item_acc_ref,
):
    layer = layer_ref[0]
    tiles, words = mask_ref.shape[:2]
    shards, half_blocks = own_ref.shape[:2]
    per_shard = tiles // shards

    @pl.when(pl.program_id(0) == 0)
    def _():
        for b in range(user_t_ref.shape[0]):
            block = user_ref[:, b * TB:(b + 1) * TB].astype(F32)
            user_t_ref[b] = block.T.astype(BF16)

    item_acc_ref[...] = jnp.zeros_like(item_acc_ref)

    bit = jnp.left_shift(jnp.int32(1), lax.broadcasted_iota(jnp.int32, (8, TB), 0))
    for t in range(tiles):
        b, c = tile_place(rows_ref, cols_ref, t, tiles)
        item = item_block(own_ref, other_ref, layer, t // per_shard, c)
        scores = jnp.dot(user_t_ref[b], item, preferred_element_type=F32)
        difference = scores - rating_ref[t].astype(F32)
        parts = []
        for w in range(words):
            word = jnp.broadcast_to(mask_ref[t, w:w + 1, :], (8, TB))
            parts.append(jnp.where((word & bit) != 0, difference[w * 8:(w + 1) * 8], 0.0))
        residual_ref[t] = jnp.concatenate(parts, axis=0).astype(BF16)

    for t in range(tiles):
        b, c = tile_place(rows_ref, cols_ref, t, tiles)
        user = user_ref[:, pl.ds(pl.multiple_of(b * TB, TB), TB)]
        item_acc_ref[(t // per_shard) * 2 * half_blocks + c] += jnp.dot(
            user, residual_ref[t], preferred_element_type=F32
        )

    for g in range(shards):
        for j in range(half_blocks):
            at = g * 2 * half_blocks + j
            keep_ref[g, j] = item_acc_ref[at + layer * half_blocks].astype(BF16)
            send_ref[g, j] = item_acc_ref[at + (1 - layer) * half_blocks].astype(BF16)


def user_kernel(
    rows_ref, cols_ref, layer_ref, own_ref, other_ref, residual_ref, user_out_ref, user_acc_ref
):
    tiles = residual_ref.shape[0]
    per_shard = tiles // own_ref.shape[0]

    @pl.when(pl.program_id(0) == 0)
    def _():
        user_acc_ref[...] = jnp.zeros_like(user_acc_ref)

    for t in range(tiles):
        b, c = tile_place(rows_ref, cols_ref, t, tiles)
        item = item_block(own_ref, other_ref, layer_ref[0], t // per_shard, c)
        user_acc_ref[b] += lax.dot_general(
            residual_ref[t], item, (((1,), (1,)), ((), ())), preferred_element_type=F32
        )

    @pl.when(pl.program_id(0) == pl.num_programs(0) - 1)
    def _():
        for b in range(user_out_ref.shape[0]):
            user_out_ref[b] = user_acc_ref[b].T


def over_shards(shape):
    return pl.BlockSpec((shape[0] // SIDE,) + shape[1:], lambda i, *_: (i,) + (0,) * (len(shape) - 1))


def whole(shape):
    return pl.BlockSpec(shape, lambda i, *_: (0,) * len(shape))


def item_terms(places, user_factors, own, other, ratings, masks):
    _, half_blocks, rank, _ = own.shape
    tiles = ratings.shape[0] // SIDE
    return pl.pallas_call(
        item_kernel,
        grid_spec=pltpu.PrefetchScalarGridSpec(
            num_scalar_prefetch=3,
            grid=(SIDE,),
            in_specs=[whole(user_factors.shape)]
            + [over_shards(x.shape) for x in (own, other, ratings, masks)],
            out_specs=[over_shards(x.shape) for x in (own, own, ratings)],
            scratch_shapes=[
                pltpu.VMEM((user_factors.shape[1] // TB, TB, rank), BF16),
                pltpu.VMEM((own.shape[0] // SIDE * 2 * half_blocks, rank, TB), F32),
            ],
        ),
        out_shape=[jax.ShapeDtypeStruct(x.shape, BF16) for x in (own, own, ratings)],
        compiler_params=pltpu.CompilerParams(vmem_limit_bytes=32 * 1024 * 1024),
        name="item_terms",
    )(*places, user_factors, own, other, ratings, masks)


def user_terms(places, own, other, residual, user_blocks):
    rank = own.shape[2]
    shape = (user_blocks, rank, TB)
    return pl.pallas_call(
        user_kernel,
        grid_spec=pltpu.PrefetchScalarGridSpec(
            num_scalar_prefetch=3,
            grid=(SIDE,),
            in_specs=[over_shards(x.shape) for x in (own, other, residual)],
            out_specs=whole(shape),
            scratch_shapes=[pltpu.VMEM((user_blocks, TB, rank), F32)],
        ),
        out_shape=jax.ShapeDtypeStruct(shape, F32),
        compiler_params=pltpu.CompilerParams(vmem_limit_bytes=32 * 1024 * 1024),
        name="user_terms",
    )(*places, own, other, residual)


def spread(block, axes):
    copies = jnp.broadcast_to(block[None], (lax.axis_size(axes),) + block.shape)
    return lax.all_to_all(copies, axes, 0, 0)


def body(user_factors, item_factors, ratings, masks, tile_rows, tile_cols):
    rank, shard_len = item_factors.shape
    half_blocks = shard_len // TB // 2
    layer = lax.axis_index("layer")
    swap = [(0, 1), (1, 0)]

    with jax.named_scope("gather_items"):
        mine = lax.dynamic_slice_in_dim(
            item_factors.reshape(rank, 2 * half_blocks, TB), layer * half_blocks, half_blocks, 1
        )
        own = spread(spread(mine.transpose(1, 0, 2), "item_z"), "item_x")
        own = own.reshape(SIDE * SIDE, half_blocks, rank, TB)
        other = lax.ppermute(own, "layer", swap)

    with jax.named_scope("tiles"):
        places = (tile_rows, tile_cols, layer.reshape(1).astype(jnp.int32))
        keep, send, residual = item_terms(places, user_factors, own, other, ratings, masks)
        user_part = user_terms(places, own, other, residual, user_factors.shape[1] // TB)

    with jax.named_scope("scatter_items"):
        received = lax.ppermute(send, "layer", swap)
        received, user_part = lax.optimization_barrier((received, user_part))
        both = (keep.astype(F32) + received.astype(F32)).astype(BF16)
        both = both.reshape(SIDE, SIDE, half_blocks, rank, TB).transpose(2, 0, 1, 3, 4)
        both = both.reshape(half_blocks * SIDE, SIDE, rank, TB)
        part = lax.all_to_all(both, ("user_y", "item_x"), 0, 0)
        part = part.astype(F32).sum(0).astype(BF16)

    with jax.named_scope("sum_along_z"):
        copies = jnp.broadcast_to(part[None], (SIDE,) + part.shape)
        copies = copies.reshape((SIDE * SIDE,) + part.shape[1:])
        part = lax.all_to_all(copies, ("user_z", "item_z"), 0, 0).astype(F32).sum(0)

    with jax.named_scope("join"):
        item_half = spread(part, "user_y")
        joined = lax.all_gather(jnp.concatenate([item_half, user_part], axis=0), "layer")
        item_total = joined[:, :half_blocks].reshape(2 * half_blocks, rank, TB)
        user_total = joined[0, half_blocks:] + joined[1, half_blocks:]
        item_total = item_total.transpose(1, 0, 2).reshape(rank, shard_len)
        user_total = user_total.transpose(1, 0, 2).reshape(user_factors.shape)
        grad_users = LOSS_SCALE * user_total + DECAY * user_factors.astype(F32)
        grad_items = LOSS_SCALE * item_total + DECAY * item_factors.astype(F32)
    return (grad_users, grad_items)


def solution(mesh):
    fine = Mesh(
        mesh.devices.reshape(SIDE, SIDE, SIDE, SIDE, 2),
        ("user_y", "user_z", "item_x", "item_z", "layer"),
    )
    users = ("user_y", "user_z")
    items = ("item_x", "item_z")
    everywhere = users + items + ("layer",)
    return jax.shard_map(
        body,
        mesh=fine,
        in_specs=(
            P(None, users + items),
            P(None, items),
            P(everywhere, None, None),
            P(everywhere, None, None),
            P(everywhere),
            P(everywhere),
        ),
        out_specs=(P(None, users + items), P(None, items)),
        check_vma=False,
    )
```

time: 117 us -> 116 us (level)
  waiting for transfers between devices: 4.53 us -> 2.27 us
  Pallas kernels: 6.3 us -> 7.49 us
    ppermute x1, waiting for transfers between devices: 2.26 us -> 0.01 us  [body(): received = lax.ppermute(send, 'layer', swap)]
    pallas_call x1 -> x2, Pallas kernels: 6.3 us -> 7.49 us  [the longest x1 4.76 us: item_terms(): pl.pallas_call(item_kernel, grid_spec=pltpu.PrefetchScalarGridSpec(num_sc...]
  transfers between devices with their start and end apart: 2 -> 2, of which waited for: 2 -> 1; matrix products, arithmetic and copies ran while one was open for 0% -> 0% of each run, Pallas kernels for 0% -> 2%
where the time goes in v4:
time: 116 us
  blocking collectives  92.3 us (80%)
  starting transfers between devices  8.33 us (7%)
  Pallas kernels  7.49 us (6%)
  local copies, waits for them, and re-layouts  2.82 us (2%)
  waiting for transfers between devices  2.27 us (2%)
  other arithmetic  2.13 us (2%)
    all_to_all x3, blocking collectives, spread(): return lax.all_to_all(copies, axes, 0, 0)  36.3 us
    all_to_all x1, blocking collectives, body(): part = lax.all_to_all(copies, ('user_z', 'item_z'), 0, 0).astype(F32).sum(0)  24.9 us
    all_to_all x1, blocking collectives, body(): part = lax.all_to_all(both, ('user_y', 'item_x'), 0, 0)  21.3 us
    all_gather x1, blocking collectives, body(): lax.all_gather(jnp.concatenate([item_half, user_part], axis=0), 'layer')  9.72 us
    ppermute x1, starting transfers between devices, body(): other = lax.ppermute(own, 'layer', swap)  6.04 us
    pallas_call x1, Pallas kernels, item_terms(): pl.pallas_call(item_kernel, grid_spec=pltpu.PrefetchScalarGridSpec(num_sc...  4.76 us
    pallas_call x1, Pallas kernels, user_terms(): pl.pallas_call(user_kernel, grid_spec=pltpu.PrefetchScalarGridSpec(num_sc...  2.74 us
  transfers between devices with their start and end apart: 2, of which 1 were waited for; matrix products, arithmetic and copies ran while one was open for 0% of the time, Pallas kernels for 2%

profile of v4, /device:TPU:1, one launch (start us, length us, event | category | flops | bytes accessed | tf_op | source)
XLA Modules:
  0.0 116.1 jit_solution(8461706985056368596)
XLA Ops:
  0.6 0.9 copy.24
  1.6 0.0 copy-start
  1.6 0.0 copy-start.2
  1.7 0.0 copy-start.3
  1.7 0.0 copy-start.4
  1.7 12.5 %all_to_all.25 = bf16[4,4,64,128]{3,2,1,0:T(8,128)(2,1)S(1)} all-to-all(bf16[4,4,64,128]{3,2,1,0:T(8,128)(2,1)S(1)} %broadcast_in_dim.8), channel_id=1, replica_groups=mesh['user_y'=4,'user_z'=4,'item_x'=4,'item_z'=4,'layer'=2] {'item_z'}, dimensions={0} | all-to-all | bytes 524288 | tf_op jit(solution)/shard_map/gather_items/all_to_all | solution.py:144
  14.2 0.2 broadcast_in_dim.9
  14.5 16.6 %all_to_all.26 = bf16[4,4,4,64,128]{4,3,2,1,0:T(8,128)(2,1)S(1)} all-to-all(bf16[4,4,4,64,128]{4,3,2,1,0:T(8,128)(2,1)S(1)} %broadcast_in_dim.9), channel_id=1, replica_groups=mesh['user_y'=4,'user_z'=4,'item_x'=4,'item_z'=4,'layer'=2] {'item_x'}, dimensions={0} | all-to-all | bytes 2097152 | tf_op jit(solution)/shard_map/gather_items/all_to_all | solution.py:144
  31.1 6.0 %collective-permute-start = (bf16[16,4,64,128]{3,2,1,0:T(8,128)(2,1)S(1)}, bf16[16,4,64,128]{3,2,1,0:T(8,128)(2,1)S(1)}, u32[]{:S(2)}, u32[]{:S(2)}) collective-permute-start(bf16[16,4,64,128]{3,2,1,0:T(8,128)(2,1)S(1)} %bitcast.25), channel_id=1, source_target_pairs={{0,1},{1,0},{2,3},{3,2},{4,5},{5,4},{6,7},{7,6},{8,9},{9,8},{10,11... | collective-permute-start | bytes 3145736 | tf_op jit(solution)/shard_map/gather_items/ppermute | solution.py:159
  37.1 2.3 %collective-permute-done.other_ref = bf16[16,4,64,128]{3,2,1,0:T(8,128)(2,1)S(1)} collective-permute-done((bf16[16,4,64,128]{3,2,1,0:T(8,128)(2,1)S(1)}, bf16[16,4,64,128]{3,2,1,0:T(8,128)(2,1)S(1)}, u32[]{:S(2)}, u32[]{:S(2)}) %collective-permute-start) | collective-permute-done | bytes 1048608 | tf_op jit(solution)/shard_map/gather_items/ppermute | solution.py:159
  39.4 0.0 copy-done
  39.4 0.0 copy-done.2
  39.4 0.0 copy-done.3
  39.4 0.0 copy-done.4
  39.4 0.0 copy-start.1
  39.4 1.2 %copy-done.1 = s32[128,16,128]{2,1,0:T(8,128)S(1)} copy-done((s32[128,16,128]{2,1,0:T(8,128)S(1)}, s32[128,16,128]{2,1,0:T(8,128)}, u32[]{:S(2)}) %copy-start.1) | copy-done | bytes 1048600
  40.6 4.8 %item_terms.1 = (bf16[16,4,64,128]{3,2,1,0:T(8,128)(2,1)S(1)}, bf16[16,4,64,128]{3,2,1,0:T(8,128)(2,1)S(1)}, bf16[128,128,128]{2,1,0:T(8,128)(2,1)S(1)}) custom-call(s32[128]{0:T(128)S(1)} %copy-done.3, s32[128]{0:T(128)S(1)} %copy-done.4, s32[1]{0:T(128)} %bitcast.layer_ref, bf16[64,512]{1,0:T(8,128)(2,1)S(1)} %copy-done.2, ...), custom_call_target="tpu_custom_call" | custom-call | tf_op jit(solution)/shard_map/tiles/item_terms/pallas_call | solution.py:105
  45.4 2.3 %collective-permute-start.1 = (bf16[16,4,64,128]{3,2,1,0:T(8,128)(2,1)S(1)}, bf16[16,4,64,128]{3,2,1,0:T(8,128)(2,1)S(1)}, u32[]{:S(2)}, u32[]{:S(2)}) collective-permute-start(bf16[16,4,64,128]{3,2,1,0:T(8,128)(2,1)S(1)} %get-tuple-element.8), channel_id=1, source_target_pairs={{0,1},{1,0},{2,3},{3,2},{4,5},{5,4},{6,7},{7,6},{8,9},{9,8},{10,11... | collective-permute-start | bytes 3145736 | tf_op jit(solution)/shard_map/scatter_items/ppermute | solution.py:167
  47.7 2.7 %user_terms.1 = f32[4,64,128]{2,1,0:T(8,128)S(1)} custom-call(s32[128]{0:T(128)S(1)} %copy-done.3, s32[128]{0:T(128)S(1)} %copy-done.4, s32[1]{0:T(128)} %bitcast.layer_ref, bf16[16,4,64,128]{3,2,1,0:T(8,128)(2,1)S(1)} %bitcast.27, bf16[16,4,64,128]{3,2,1,0:T(8,128)(2,1)S(1)} %collective-permute-done.other_ref, ...), custom_call_target="tpu_custom_call" | custom-call | tf_op jit(solution)/shard_map/tiles/user_terms/pallas_call | solution.py:127
  50.4 0.0 collective-permute-done.1
  50.5 0.4 add_convert_fusion
  50.9 0.1 copy.20
  51.0 21.3 %all_to_all.27 = bf16[16,4,64,128]{3,2,1,0:T(8,128)(2,1)S(1)} all-to-all(bf16[16,4,64,128]{3,2,1,0:T(8,128)(2,1)S(1)} %bitcast.29), channel_id=1, replica_groups=mesh['user_y'=4,'user_z'=4,'item_x'=4,'item_z'=4,'layer'=2] {'user_y','i..., dimensions={0} | all-to-all | bytes 2097152 | tf_op jit(solution)/shard_map/scatter_items/all_to_all | solution.py:172
  72.2 0.2 reduce_sum.21
  72.5 0.0 copy-start.5
  72.5 24.9 %all_to_all.28 = bf16[16,64,128]{2,1,0:T(8,128)(2,1)S(1)} all-to-all(bf16[16,64,128]{2,1,0:T(8,128)(2,1)S(1)} %bitcast.32), channel_id=1, replica_groups=mesh['user_y'=4,'user_z'=4,'item_x'=4,'item_z'=4,'layer'=2] {'user_z','i..., dimensions={0} | all-to-all | bytes 524288 | tf_op jit(solution)/shard_map/sum_along_z/all_to_all | solution.py:178
  97.5 7.2 %all_to_all.29 = f32[4,64,128]{2,1,0:T(8,128)S(1)} all-to-all(f32[4,64,128]{2,1,0:T(8,128)S(1)} %broadcast_in_dim.11), channel_id=1, replica_groups=mesh['user_y'=4,'user_z'=4,'item_x'=4,'item_z'=4,'layer'=2] {'user_y'}, dimensions={0} | all-to-all | bytes 262144 | tf_op jit(solution)/shard_map/join/all_to_all | solution.py:144
  104.7 9.7 %all-gather = f32[16,64,128]{2,1,0:T(8,128)S(1)} all-gather(f32[8,64,128]{2,1,0:T(8,128)S(1)} %pad_maximum_fusion), channel_id=2, replica_groups=mesh['user_y'=4,'user_z'=4,'item_x'=4,'item_z'=4,'layer'=2] {'layer'}, dimensions={0}, use_global_device_ids=true | all-gather | bytes 786432 | tf_op jit(solution)/shard_map/join/all_gather | solution.py:182
  114.5 0.7 bitcast_add_fusion.1
  115.2 0.2 copy.22
  115.3 0.0 copy-done.5
  115.3 0.8 bitcast_add_fusion
  (8 shorter events, 0.2 us)
Async XLA Ops:
  1.6 37.8 %copy-start = (bf16[128,128,128]{2,1,0:T(8,128)(2,1)S(1)}, bf16[128,128,128]{2,1,0:T(8,128)(2,1)}, u32[]{:S(2)}) copy-start(bf16[128,128,128]{2,1,0:T(8,128)(2,1)} %rating_ref.1) | copy-start | bytes 12582916
  1.6 37.8 %copy-start.2 = (bf16[64,512]{1,0:T(8,128)(2,1)S(1)}, bf16[64,512]{1,0:T(8,128)(2,1)}, u32[]{:S(2)}) copy-start(bf16[64,512]{1,0:T(8,128)(2,1)} %user_ref.1) | copy-start | bytes 196612
  1.7 37.8 %copy-start.3 = (s32[128]{0:T(128)S(1)}, s32[128]{0:T(128)}, u32[]{:S(2)}) copy-start(s32[128]{0:T(128)} %rows_ref.3) | copy-start | bytes 1540
  1.7 37.7 %copy-start.4 = (s32[128]{0:T(128)S(1)}, s32[128]{0:T(128)}, u32[]{:S(2)}) copy-start(s32[128]{0:T(128)} %cols_ref.3) | copy-start | bytes 1540
  31.1 8.3 %collective-permute-start = (bf16[16,4,64,128]{3,2,1,0:T(8,128)(2,1)S(1)}, bf16[16,4,64,128]{3,2,1,0:T(8,128)(2,1)S(1)}, u32[]{:S(2)}, u32[]{:S(2)}) collective-permute-start(bf16[16,4,64,128]{3,2,1,0:T(8,128)(2,1)S(1)} %bitcast.25), channel_id=1, source_target_pairs={{0,1},{1,0},{2,3},{3,2},{4,5},{5,4},{6,7},{7,6},{8,9},{9,8},{10,11... | collective-permute-start | bytes 3145736 | tf_op jit(solution)/shard_map/gather_items/ppermute | solution.py:159
  39.4 1.2 %copy-start.1 = (s32[128,16,128]{2,1,0:T(8,128)S(1)}, s32[128,16,128]{2,1,0:T(8,128)}, u32[]{:S(2)}) copy-start(s32[128,16,128]{2,1,0:T(8,128)} %mask_ref.1) | copy-start | bytes 3145732
  45.4 5.0 %collective-permute-start.1 = (bf16[16,4,64,128]{3,2,1,0:T(8,128)(2,1)S(1)}, bf16[16,4,64,128]{3,2,1,0:T(8,128)(2,1)S(1)}, u32[]{:S(2)}, u32[]{:S(2)}) collective-permute-start(bf16[16,4,64,128]{3,2,1,0:T(8,128)(2,1)S(1)} %get-tuple-element.8), channel_id=1, source_target_pairs={{0,1},{1,0},{2,3},{3,2},{4,5},{5,4},{6,7},{7,6},{8,9},{9,8},{10,11... | collective-permute-start | bytes 3145736 | tf_op jit(solution)/shard_map/scatter_items/ppermute | solution.py:167
  72.5 42.8 %copy-start.5 = (bf16[64,1024]{1,0:T(8,128)(2,1)S(1)}, bf16[64,1024]{1,0:T(8,128)(2,1)}, u32[]{:S(2)}) copy-start(bf16[64,1024]{1,0:T(8,128)(2,1)} %param.7) | copy-start | bytes 393220

commit v5 on v4

--- a/solution.py
+++ b/solution.py
@@ -26,19 +26,13 @@
 
 
 def item_kernel(
-    rows_ref, cols_ref, layer_ref, user_ref, own_ref, other_ref, rating_ref, mask_ref,
-    keep_ref, send_ref, residual_ref, user_t_ref, item_acc_ref,
+    rows_ref, cols_ref, layer_ref, user_ref, user_t_ref, own_ref, other_ref, rating_ref,
+    mask_ref, keep_ref, send_ref, residual_ref, item_acc_ref,
 ):
     layer = layer_ref[0]
     tiles, words = mask_ref.shape[:2]
     shards, half_blocks = own_ref.shape[:2]
     per_shard = tiles // shards
-
-    @pl.when(pl.program_id(0) == 0)
-    def _():
-        for b in range(user_t_ref.shape[0]):
-            block = user_ref[:, b * TB:(b + 1) * TB].astype(F32)
-            user_t_ref[b] = block.T.astype(BF16)
 
     item_acc_ref[...] = jnp.zeros_like(item_acc_ref)
 
@@ -99,7 +93,7 @@
     return pl.BlockSpec(shape, lambda i, *_: (0,) * len(shape))
 
 
-def item_terms(places, user_factors, own, other, ratings, masks):
+def item_terms(places, user_factors, user_t, own, other, ratings, masks):
     _, half_blocks, rank, _ = own.shape
     tiles = ratings.shape[0] // SIDE
     return pl.pallas_call(
@@ -107,18 +101,17 @@
         grid_spec=pltpu.PrefetchScalarGridSpec(
             num_scalar_prefetch=3,
             grid=(SIDE,),
-            in_specs=[whole(user_factors.shape)]
+            in_specs=[whole(user_factors.shape), whole(user_t.shape)]
             + [over_shards(x.shape) for x in (own, other, ratings, masks)],
             out_specs=[over_shards(x.shape) for x in (own, own, ratings)],
             scratch_shapes=[
-                pltpu.VMEM((user_factors.shape[1] // TB, TB, rank), BF16),
                 pltpu.VMEM((own.shape[0] // SIDE * 2 * half_blocks, rank, TB), F32),
             ],
         ),
         out_shape=[jax.ShapeDtypeStruct(x.shape, BF16) for x in (own, own, ratings)],
-        compiler_params=pltpu.CompilerParams(vmem_limit_bytes=32 * 1024 * 1024),
+        compiler_params=pltpu.CompilerParams(vmem_limit_bytes=16 * 1024 * 1024),
         name="item_terms",
-    )(*places, user_factors, own, other, ratings, masks)
+    )(*places, user_factors, user_t, own, other, ratings, masks)
 
 
 def user_terms(places, own, other, residual, user_blocks):
@@ -134,9 +127,29 @@
             scratch_shapes=[pltpu.VMEM((user_blocks, TB, rank), F32)],
         ),
         out_shape=jax.ShapeDtypeStruct(shape, F32),
-        compiler_params=pltpu.CompilerParams(vmem_limit_bytes=32 * 1024 * 1024),
+        compiler_params=pltpu.CompilerParams(vmem_limit_bytes=16 * 1024 * 1024),
         name="user_terms",
     )(*places, own, other, residual)
+
+
+def ready_kernel(user_ref, masks_ref, user_t_ref, bits_ref):
+    for b in range(user_t_ref.shape[0]):
+        block = user_ref[:, b * TB:(b + 1) * TB].astype(F32)
+        user_t_ref[b] = block.T.astype(BF16)
+    bits_ref[...] = masks_ref[...]
+
+
+def ready(user_factors, masks):
+    rank, users = user_factors.shape
+    return pl.pallas_call(
+        ready_kernel,
+        out_shape=(
+            jax.ShapeDtypeStruct((users // TB, TB, rank), BF16),
+            jax.ShapeDtypeStruct(masks.shape, masks.dtype),
+        ),
+        compiler_params=pltpu.CompilerParams(vmem_limit_bytes=8 * 1024 * 1024),
+        name="ready",
+    )(user_factors, masks)
 
 
 def spread(block, axes):
@@ -157,10 +170,12 @@
         own = spread(spread(mine.transpose(1, 0, 2), "item_z"), "item_x")
         own = own.reshape(SIDE * SIDE, half_blocks, rank, TB)
         other = lax.ppermute(own, "layer", swap)
+        user_t, bits = ready(user_factors, masks)
+        other, user_t, bits = lax.optimization_barrier((other, user_t, bits))
 
     with jax.named_scope("tiles"):
         places = (tile_rows, tile_cols, layer.reshape(1).astype(jnp.int32))
-        keep, send, residual = item_terms(places, user_factors, own, other, ratings, masks)
+        keep, send, residual = item_terms(places, user_factors, user_t, own, other, ratings, bits)
         user_part = user_terms(places, own, other, residual, user_factors.shape[1] // TB)
 
     with jax.named_scope("scatter_items"):

time: 116 us -> 115 us (level)
  local copies, waits for them, and re-layouts: 2.82 us -> 1.6 us
    unnamed x13, local copies, waits for them, and re-layouts: 2.18 us -> 0.96 us
where the time goes in v5:
time: 115 us
  blocking collectives  92.4 us (80%)
  starting transfers between devices  8.35 us (7%)
  Pallas kernels  7.67 us (7%)
  other arithmetic  2.16 us (2%)
  waiting for transfers between devices  2.14 us (2%)
  local copies, waits for them, and re-layouts  1.6 us (1%)
    all_to_all x3, blocking collectives, spread(): return lax.all_to_all(copies, axes, 0, 0)  36.4 us
    all_to_all x1, blocking collectives, body(): part = lax.all_to_all(copies, ('user_z', 'item_z'), 0, 0).astype(F32).sum(0)  24.9 us
    all_to_all x1, blocking collectives, body(): part = lax.all_to_all(both, ('user_y', 'item_x'), 0, 0)  21.3 us
    all_gather x1, blocking collectives, body(): lax.all_gather(jnp.concatenate([item_half, user_part], axis=0), 'layer')  9.72 us
    ppermute x1, starting transfers between devices, body(): other = lax.ppermute(own, 'layer', swap)  6.04 us
    pallas_call x1, Pallas kernels, item_terms(): pl.pallas_call(item_kernel, grid_spec=pltpu.PrefetchScalarGridSpec(num_sc...  4.82 us
    pallas_call x1, Pallas kernels, user_terms(): pl.pallas_call(user_kernel, grid_spec=pltpu.PrefetchScalarGridSpec(num_sc...  2.74 us
    ppermute x1, starting transfers between devices, body(): received = lax.ppermute(send, 'layer', swap)  2.31 us
  transfers between devices with their start and end apart: 2, of which 1 were waited for; matrix products, arithmetic and copies ran while one was open for 0% of the time, Pallas kernels for 2%

profile of v5, /device:TPU:1, one launch (start us, length us, event | category | flops | bytes accessed | tf_op | source)
XLA Modules:
  0.0 115.1 jit_solution(2974233613713002323)
XLA Ops:
  0.6 0.9 copy.24
  1.6 0.0 copy-start.1
  1.6 0.0 copy-start.2
  1.7 12.4 %all_to_all.25 = bf16[4,4,64,128]{3,2,1,0:T(8,128)(2,1)S(1)} all-to-all(bf16[4,4,64,128]{3,2,1,0:T(8,128)(2,1)S(1)} %broadcast_in_dim.8), channel_id=1, replica_groups=mesh['user_y'=4,'user_z'=4,'item_x'=4,'item_z'=4,'layer'=2] {'item_z'}, dimensions={0} | all-to-all | bytes 524288 | tf_op jit(solution)/shard_map/gather_items/all_to_all | solution.py:157
  14.1 0.0 copy-start
  14.1 0.0 copy-start.3
  14.1 0.0 copy-start.4
  14.1 0.2 broadcast_in_dim.9
  14.3 16.9 %all_to_all.26 = bf16[4,4,4,64,128]{4,3,2,1,0:T(8,128)(2,1)S(1)} all-to-all(bf16[4,4,4,64,128]{4,3,2,1,0:T(8,128)(2,1)S(1)} %broadcast_in_dim.9), channel_id=1, replica_groups=mesh['user_y'=4,'user_z'=4,'item_x'=4,'item_z'=4,'layer'=2] {'item_x'}, dimensions={0} | all-to-all | bytes 2097152 | tf_op jit(solution)/shard_map/gather_items/all_to_all | solution.py:157
  31.2 6.0 %collective-permute-start = (bf16[16,4,64,128]{3,2,1,0:T(8,128)(2,1)S(1)}, bf16[16,4,64,128]{3,2,1,0:T(8,128)(2,1)S(1)}, u32[]{:S(2)}, u32[]{:S(2)}) collective-permute-start(bf16[16,4,64,128]{3,2,1,0:T(8,128)(2,1)S(1)} %bitcast.25), channel_id=1, source_target_pairs={{0,1},{1,0},{2,3},{3,2},{4,5},{5,4},{6,7},{7,6},{8,9},{9,8},{10,11... | collective-permute-start | bytes 3145736 | tf_op jit(solution)/shard_map/gather_items/ppermute | solution.py:172
  37.3 0.0 copy-done.1
  37.3 0.0 copy-done.2
  37.3 0.1 ready.1
  37.4 2.1 %collective-permute-done.other_ref = bf16[16,4,64,128]{3,2,1,0:T(8,128)(2,1)S(1)} collective-permute-done((bf16[16,4,64,128]{3,2,1,0:T(8,128)(2,1)S(1)}, bf16[16,4,64,128]{3,2,1,0:T(8,128)(2,1)S(1)}, u32[]{:S(2)}, u32[]{:S(2)}) %collective-permute-start) | collective-permute-done | bytes 1048608 | tf_op jit(solution)/shard_map/gather_items/ppermute | solution.py:172
  39.5 0.0 copy-done
  39.5 0.0 copy-done.3
  39.5 0.0 copy-done.4
  39.5 4.8 %item_terms.1 = (bf16[16,4,64,128]{3,2,1,0:T(8,128)(2,1)S(1)}, bf16[16,4,64,128]{3,2,1,0:T(8,128)(2,1)S(1)}, bf16[128,128,128]{2,1,0:T(8,128)(2,1)S(1)}) custom-call(s32[128]{0:T(128)S(1)} %copy-done.3, s32[128]{0:T(128)S(1)} %copy-done.4, s32[1]{0:T(128)} %bitcast.layer_ref, bf16[64,512]{1,0:T(8,128)(2,1)S(1)} %copy-done.2, ...), custom_call_target="tpu_custom_call" | custom-call | tf_op jit(solution)/shard_map/tiles/item_terms/pallas_call | solution.py:99
  44.4 2.3 %collective-permute-start.1 = (bf16[16,4,64,128]{3,2,1,0:T(8,128)(2,1)S(1)}, bf16[16,4,64,128]{3,2,1,0:T(8,128)(2,1)S(1)}, u32[]{:S(2)}, u32[]{:S(2)}) collective-permute-start(bf16[16,4,64,128]{3,2,1,0:T(8,128)(2,1)S(1)} %get-tuple-element.18), channel_id=1, source_target_pairs={{0,1},{1,0},{2,3},{3,2},{4,5},{5,4},{6,7},{7,6},{8,9},{9,8},{10,11... | collective-permute-start | bytes 3145736 | tf_op jit(solution)/shard_map/scatter_items/ppermute | solution.py:182
  46.7 2.7 %user_terms.1 = f32[4,64,128]{2,1,0:T(8,128)S(1)} custom-call(s32[128]{0:T(128)S(1)} %copy-done.3, s32[128]{0:T(128)S(1)} %copy-done.4, s32[1]{0:T(128)} %bitcast.layer_ref, bf16[16,4,64,128]{3,2,1,0:T(8,128)(2,1)S(1)} %bitcast.27, bf16[16,4,64,128]{3,2,1,0:T(8,128)(2,1)S(1)} %collective-permute-done.other_ref, ...), custom_call_target="tpu_custom_call" | custom-call | tf_op jit(solution)/shard_map/tiles/user_terms/pallas_call | solution.py:120
  49.4 0.0 collective-permute-done.1
  49.4 0.4 add_convert_fusion
  49.9 0.1 copy.20
  50.0 21.3 %all_to_all.27 = bf16[16,4,64,128]{3,2,1,0:T(8,128)(2,1)S(1)} all-to-all(bf16[16,4,64,128]{3,2,1,0:T(8,128)(2,1)S(1)} %bitcast.29), channel_id=1, replica_groups=mesh['user_y'=4,'user_z'=4,'item_x'=4,'item_z'=4,'layer'=2] {'user_y','i..., dimensions={0} | all-to-all | bytes 2097152 | tf_op jit(solution)/shard_map/scatter_items/all_to_all | solution.py:187
  71.2 0.2 reduce_sum.21
  71.5 0.0 copy-start.5
  71.5 24.9 %all_to_all.28 = bf16[16,64,128]{2,1,0:T(8,128)(2,1)S(1)} all-to-all(bf16[16,64,128]{2,1,0:T(8,128)(2,1)S(1)} %bitcast.32), channel_id=1, replica_groups=mesh['user_y'=4,'user_z'=4,'item_x'=4,'item_z'=4,'layer'=2] {'user_z','i..., dimensions={0} | all-to-all | bytes 524288 | tf_op jit(solution)/shard_map/sum_along_z/all_to_all | solution.py:193
  96.5 7.2 %all_to_all.29 = f32[4,64,128]{2,1,0:T(8,128)S(1)} all-to-all(f32[4,64,128]{2,1,0:T(8,128)S(1)} %broadcast_in_dim.11), channel_id=1, replica_groups=mesh['user_y'=4,'user_z'=4,'item_x'=4,'item_z'=4,'layer'=2] {'user_y'}, dimensions={0} | all-to-all | bytes 262144 | tf_op jit(solution)/shard_map/join/all_to_all | solution.py:157
  103.7 9.7 %all-gather = f32[16,64,128]{2,1,0:T(8,128)S(1)} all-gather(f32[8,64,128]{2,1,0:T(8,128)S(1)} %pad_maximum_fusion), channel_id=2, replica_groups=mesh['user_y'=4,'user_z'=4,'item_x'=4,'item_z'=4,'layer'=2] {'layer'}, dimensions={0}, use_global_device_ids=true | all-gather | bytes 786432 | tf_op jit(solution)/shard_map/join/all_gather | solution.py:197
  113.4 0.7 bitcast_add_fusion.1
  114.2 0.2 copy.22
  114.3 0.0 copy-done.5
  114.3 0.8 bitcast_add_fusion
  (8 shorter events, 0.2 us)
Async XLA Ops:
  1.6 35.6 %copy-start.1 = (s32[128,16,128]{2,1,0:T(8,128)S(1)}, s32[128,16,128]{2,1,0:T(8,128)}, u32[]{:S(2)}) copy-start(s32[128,16,128]{2,1,0:T(8,128)} %masks_ref.1) | copy-start | bytes 3145732
  1.6 35.6 %copy-start.2 = (bf16[64,512]{1,0:T(8,128)(2,1)S(1)}, bf16[64,512]{1,0:T(8,128)(2,1)}, u32[]{:S(2)}) copy-start(bf16[64,512]{1,0:T(8,128)(2,1)} %user_ref.3) | copy-start | bytes 196612
  14.1 25.5 %copy-start = (bf16[128,128,128]{2,1,0:T(8,128)(2,1)S(1)}, bf16[128,128,128]{2,1,0:T(8,128)(2,1)}, u32[]{:S(2)}) copy-start(bf16[128,128,128]{2,1,0:T(8,128)(2,1)} %rating_ref.1) | copy-start | bytes 12582916
  14.1 25.5 %copy-start.3 = (s32[128]{0:T(128)S(1)}, s32[128]{0:T(128)}, u32[]{:S(2)}) copy-start(s32[128]{0:T(128)} %rows_ref.3) | copy-start | bytes 1540
  14.1 25.5 %copy-start.4 = (s32[128]{0:T(128)S(1)}, s32[128]{0:T(128)}, u32[]{:S(2)}) copy-start(s32[128]{0:T(128)} %cols_ref.3) | copy-start | bytes 1540
  31.2 8.3 %collective-permute-start = (bf16[16,4,64,128]{3,2,1,0:T(8,128)(2,1)S(1)}, bf16[16,4,64,128]{3,2,1,0:T(8,128)(2,1)S(1)}, u32[]{:S(2)}, u32[]{:S(2)}) collective-permute-start(bf16[16,4,64,128]{3,2,1,0:T(8,128)(2,1)S(1)} %bitcast.25), channel_id=1, source_target_pairs={{0,1},{1,0},{2,3},{3,2},{4,5},{5,4},{6,7},{7,6},{8,9},{9,8},{10,11... | collective-permute-start | bytes 3145736 | tf_op jit(solution)/shard_map/gather_items/ppermute | solution.py:172
  44.4 5.1 %collective-permute-start.1 = (bf16[16,4,64,128]{3,2,1,0:T(8,128)(2,1)S(1)}, bf16[16,4,64,128]{3,2,1,0:T(8,128)(2,1)S(1)}, u32[]{:S(2)}, u32[]{:S(2)}) collective-permute-start(bf16[16,4,64,128]{3,2,1,0:T(8,128)(2,1)S(1)} %get-tuple-element.18), channel_id=1, source_target_pairs={{0,1},{1,0},{2,3},{3,2},{4,5},{5,4},{6,7},{7,6},{8,9},{9,8},{10,11... | collective-permute-start | bytes 3145736 | tf_op jit(solution)/shard_map/scatter_items/ppermute | solution.py:182
  71.5 42.8 %copy-start.5 = (bf16[64,1024]{1,0:T(8,128)(2,1)S(1)}, bf16[64,1024]{1,0:T(8,128)(2,1)}, u32[]{:S(2)}) copy-start(bf16[64,1024]{1,0:T(8,128)(2,1)} %param.7) | copy-start | bytes 393220

commit v6 on v5

--- a/solution.py
+++ b/solution.py
@@ -21,8 +21,9 @@
 
 def item_block(own_ref, other_ref, layer, shard, c):
     half_blocks = own_ref.shape[1]
-    at = c % half_blocks
-    return jnp.where(c // half_blocks == layer, own_ref[shard, at], other_ref[shard, at])
+    side = (c >= half_blocks).astype(jnp.int32)
+    at = c - half_blocks * side
+    return jnp.where(side == layer, own_ref[shard, at], other_ref[shard, at])
 
 
 def item_kernel(
@@ -182,9 +183,9 @@
         received = lax.ppermute(send, "layer", swap)
         received, user_part = lax.optimization_barrier((received, user_part))
         both = (keep.astype(F32) + received.astype(F32)).astype(BF16)
-        both = both.reshape(SIDE, SIDE, half_blocks, rank, TB).transpose(2, 0, 1, 3, 4)
+        both = both.reshape(SIDE, SIDE, half_blocks, rank, TB).transpose(0, 2, 1, 3, 4)
         both = both.reshape(half_blocks * SIDE, SIDE, rank, TB)
-        part = lax.all_to_all(both, ("user_y", "item_x"), 0, 0)
+        part = lax.all_to_all(both, ("item_x", "user_y"), 0, 0)
         part = part.astype(F32).sum(0).astype(BF16)
 
     with jax.named_scope("sum_along_z"):

time: 115 us -> 115 us (level)
  no operation moved by 1% of the time
where the time goes in v6:
time: 115 us
  blocking collectives  92.2 us (80%)
  starting transfers between devices  8.34 us (7%)
  Pallas kernels  7.37 us (6%)
  other arithmetic  2.16 us (2%)
  waiting for transfers between devices  2.14 us (2%)
  local copies, waits for them, and re-layouts  1.6 us (1%)
    all_to_all x3, blocking collectives, spread(): return lax.all_to_all(copies, axes, 0, 0)  36.6 us
    all_to_all x1, blocking collectives, body(): part = lax.all_to_all(copies, ('user_z', 'item_z'), 0, 0).astype(F32).sum(0)  24.9 us
    all_to_all x1, blocking collectives, body(): part = lax.all_to_all(both, ('item_x', 'user_y'), 0, 0)  20.5 us
    all_gather x1, blocking collectives, body(): lax.all_gather(jnp.concatenate([item_half, user_part], axis=0), 'layer')  10.2 us
    ppermute x1, starting transfers between devices, body(): other = lax.ppermute(own, 'layer', swap)  6.04 us
    pallas_call x1, Pallas kernels, item_terms(): pl.pallas_call(item_kernel, grid_spec=pltpu.PrefetchScalarGridSpec(num_sc...  4.71 us
    pallas_call x1, Pallas kernels, user_terms(): pl.pallas_call(user_kernel, grid_spec=pltpu.PrefetchScalarGridSpec(num_sc...  2.56 us
  transfers between devices with their start and end apart: 2, of which 1 were waited for; matrix products, arithmetic and copies ran while one was open for 0% of the time, Pallas kernels for 2%

profile of v6, /device:TPU:1, one launch (start us, length us, event | category | flops | bytes accessed | tf_op | source)
XLA Modules:
  0.0 114.6 jit_solution(10003672055740945565)
XLA Ops:
  0.6 0.9 copy.24
  1.6 0.0 copy-start.1
  1.6 0.0 copy-start.2
  1.7 12.4 %all_to_all.25 = bf16[4,4,64,128]{3,2,1,0:T(8,128)(2,1)S(1)} all-to-all(bf16[4,4,64,128]{3,2,1,0:T(8,128)(2,1)S(1)} %broadcast_in_dim.8), channel_id=1, replica_groups=mesh['user_y'=4,'user_z'=4,'item_x'=4,'item_z'=4,'layer'=2] {'item_z'}, dimensions={0} | all-to-all | bytes 524288 | tf_op jit(solution)/shard_map/gather_items/all_to_all | solution.py:158
  14.1 0.0 copy-start
  14.1 0.0 copy-start.3
  14.1 0.0 copy-start.4
  14.1 0.2 broadcast_in_dim.9
  14.3 16.9 %all_to_all.26 = bf16[4,4,4,64,128]{4,3,2,1,0:T(8,128)(2,1)S(1)} all-to-all(bf16[4,4,4,64,128]{4,3,2,1,0:T(8,128)(2,1)S(1)} %broadcast_in_dim.9), channel_id=1, replica_groups=mesh['user_y'=4,'user_z'=4,'item_x'=4,'item_z'=4,'layer'=2] {'item_x'}, dimensions={0} | all-to-all | bytes 2097152 | tf_op jit(solution)/shard_map/gather_items/all_to_all | solution.py:158
  31.2 6.0 %collective-permute-start = (bf16[16,4,64,128]{3,2,1,0:T(8,128)(2,1)S(1)}, bf16[16,4,64,128]{3,2,1,0:T(8,128)(2,1)S(1)}, u32[]{:S(2)}, u32[]{:S(2)}) collective-permute-start(bf16[16,4,64,128]{3,2,1,0:T(8,128)(2,1)S(1)} %bitcast.25), channel_id=1, source_target_pairs={{0,1},{1,0},{2,3},{3,2},{4,5},{5,4},{6,7},{7,6},{8,9},{9,8},{10,11... | collective-permute-start | bytes 3145736 | tf_op jit(solution)/shard_map/gather_items/ppermute | solution.py:173
  37.3 0.0 copy-done.1
  37.3 0.0 copy-done.2
  37.3 0.1 ready.1
  37.4 2.1 %collective-permute-done.other_ref = bf16[16,4,64,128]{3,2,1,0:T(8,128)(2,1)S(1)} collective-permute-done((bf16[16,4,64,128]{3,2,1,0:T(8,128)(2,1)S(1)}, bf16[16,4,64,128]{3,2,1,0:T(8,128)(2,1)S(1)}, u32[]{:S(2)}, u32[]{:S(2)}) %collective-permute-start) | collective-permute-done | bytes 1048608 | tf_op jit(solution)/shard_map/gather_items/ppermute | solution.py:173
  39.5 0.0 copy-done
  39.5 0.0 copy-done.3
  39.5 0.0 copy-done.4
  39.5 4.7 %item_terms.1 = (bf16[16,4,64,128]{3,2,1,0:T(8,128)(2,1)S(1)}, bf16[16,4,64,128]{3,2,1,0:T(8,128)(2,1)S(1)}, bf16[128,128,128]{2,1,0:T(8,128)(2,1)S(1)}) custom-call(s32[128]{0:T(128)S(1)} %copy-done.3, s32[128]{0:T(128)S(1)} %copy-done.4, s32[1]{0:T(128)} %bitcast.layer_ref, bf16[64,512]{1,0:T(8,128)(2,1)S(1)} %copy-done.2, ...), custom_call_target="tpu_custom_call" | custom-call | tf_op jit(solution)/shard_map/tiles/item_terms/pallas_call | solution.py:100
  44.2 2.3 %collective-permute-start.1 = (bf16[16,4,64,128]{3,2,1,0:T(8,128)(2,1)S(1)}, bf16[16,4,64,128]{3,2,1,0:T(8,128)(2,1)S(1)}, u32[]{:S(2)}, u32[]{:S(2)}) collective-permute-start(bf16[16,4,64,128]{3,2,1,0:T(8,128)(2,1)S(1)} %get-tuple-element.18), channel_id=1, source_target_pairs={{0,1},{1,0},{2,3},{3,2},{4,5},{5,4},{6,7},{7,6},{8,9},{9,8},{10,11... | collective-permute-start | bytes 3145736 | tf_op jit(solution)/shard_map/scatter_items/ppermute | solution.py:183
  46.5 2.6 %user_terms.1 = f32[4,64,128]{2,1,0:T(8,128)S(1)} custom-call(s32[128]{0:T(128)S(1)} %copy-done.3, s32[128]{0:T(128)S(1)} %copy-done.4, s32[1]{0:T(128)} %bitcast.layer_ref, bf16[16,4,64,128]{3,2,1,0:T(8,128)(2,1)S(1)} %bitcast.27, bf16[16,4,64,128]{3,2,1,0:T(8,128)(2,1)S(1)} %collective-permute-done.other_ref, ...), custom_call_target="tpu_custom_call" | custom-call | tf_op jit(solution)/shard_map/tiles/user_terms/pallas_call | solution.py:121
  49.1 0.0 collective-permute-done.1
  49.1 0.4 add_convert_fusion
  49.6 0.1 copy.20
  49.7 20.5 %all_to_all.27 = bf16[16,4,64,128]{3,2,1,0:T(8,128)(2,1)S(1)} all-to-all(bf16[16,4,64,128]{3,2,1,0:T(8,128)(2,1)S(1)} %bitcast.29), channel_id=1, replica_groups=mesh['user_y'=4,'user_z'=4,'item_x'=4,'item_z'=4,'layer'=2] {'item_x','u..., dimensions={0} | all-to-all | bytes 2097152 | tf_op jit(solution)/shard_map/scatter_items/all_to_all | solution.py:188
  70.2 0.2 reduce_sum.21
  70.4 0.0 copy-start.5
  70.4 24.9 %all_to_all.28 = bf16[16,64,128]{2,1,0:T(8,128)(2,1)S(1)} all-to-all(bf16[16,64,128]{2,1,0:T(8,128)(2,1)S(1)} %bitcast.32), channel_id=1, replica_groups=mesh['user_y'=4,'user_z'=4,'item_x'=4,'item_z'=4,'layer'=2] {'user_z','i..., dimensions={0} | all-to-all | bytes 524288 | tf_op jit(solution)/shard_map/sum_along_z/all_to_all | solution.py:194
  95.4 7.4 %all_to_all.29 = f32[4,64,128]{2,1,0:T(8,128)S(1)} all-to-all(f32[4,64,128]{2,1,0:T(8,128)S(1)} %broadcast_in_dim.11), channel_id=1, replica_groups=mesh['user_y'=4,'user_z'=4,'item_x'=4,'item_z'=4,'layer'=2] {'user_y'}, dimensions={0} | all-to-all | bytes 262144 | tf_op jit(solution)/shard_map/join/all_to_all | solution.py:158
  102.8 10.2 %all-gather = f32[16,64,128]{2,1,0:T(8,128)S(1)} all-gather(f32[8,64,128]{2,1,0:T(8,128)S(1)} %pad_maximum_fusion), channel_id=2, replica_groups=mesh['user_y'=4,'user_z'=4,'item_x'=4,'item_z'=4,'layer'=2] {'layer'}, dimensions={0}, use_global_device_ids=true | all-gather | bytes 786432 | tf_op jit(solution)/shard_map/join/all_gather | solution.py:198
  113.0 0.7 bitcast_add_fusion.1
  113.7 0.2 copy.22
  113.8 0.0 copy-done.5
  113.8 0.8 bitcast_add_fusion
  (8 shorter events, 0.2 us)
Async XLA Ops:
  1.6 35.6 %copy-start.1 = (s32[128,16,128]{2,1,0:T(8,128)S(1)}, s32[128,16,128]{2,1,0:T(8,128)}, u32[]{:S(2)}) copy-start(s32[128,16,128]{2,1,0:T(8,128)} %masks_ref.1) | copy-start | bytes 3145732
  1.6 35.6 %copy-start.2 = (bf16[64,512]{1,0:T(8,128)(2,1)S(1)}, bf16[64,512]{1,0:T(8,128)(2,1)}, u32[]{:S(2)}) copy-start(bf16[64,512]{1,0:T(8,128)(2,1)} %user_ref.3) | copy-start | bytes 196612
  14.1 25.5 %copy-start = (bf16[128,128,128]{2,1,0:T(8,128)(2,1)S(1)}, bf16[128,128,128]{2,1,0:T(8,128)(2,1)}, u32[]{:S(2)}) copy-start(bf16[128,128,128]{2,1,0:T(8,128)(2,1)} %rating_ref.1) | copy-start | bytes 12582916
  14.1 25.5 %copy-start.3 = (s32[128]{0:T(128)S(1)}, s32[128]{0:T(128)}, u32[]{:S(2)}) copy-start(s32[128]{0:T(128)} %rows_ref.3) | copy-start | bytes 1540
  14.1 25.5 %copy-start.4 = (s32[128]{0:T(128)S(1)}, s32[128]{0:T(128)}, u32[]{:S(2)}) copy-start(s32[128]{0:T(128)} %cols_ref.3) | copy-start | bytes 1540
  31.2 8.3 %collective-permute-start = (bf16[16,4,64,128]{3,2,1,0:T(8,128)(2,1)S(1)}, bf16[16,4,64,128]{3,2,1,0:T(8,128)(2,1)S(1)}, u32[]{:S(2)}, u32[]{:S(2)}) collective-permute-start(bf16[16,4,64,128]{3,2,1,0:T(8,128)(2,1)S(1)} %bitcast.25), channel_id=1, source_target_pairs={{0,1},{1,0},{2,3},{3,2},{4,5},{5,4},{6,7},{7,6},{8,9},{9,8},{10,11... | collective-permute-start | bytes 3145736 | tf_op jit(solution)/shard_map/gather_items/ppermute | solution.py:173
  44.2 4.9 %collective-permute-start.1 = (bf16[16,4,64,128]{3,2,1,0:T(8,128)(2,1)S(1)}, bf16[16,4,64,128]{3,2,1,0:T(8,128)(2,1)S(1)}, u32[]{:S(2)}, u32[]{:S(2)}) collective-permute-start(bf16[16,4,64,128]{3,2,1,0:T(8,128)(2,1)S(1)} %get-tuple-element.18), channel_id=1, source_target_pairs={{0,1},{1,0},{2,3},{3,2},{4,5},{5,4},{6,7},{7,6},{8,9},{9,8},{10,11... | collective-permute-start | bytes 3145736 | tf_op jit(solution)/shard_map/scatter_items/ppermute | solution.py:183
  70.4 43.4 %copy-start.5 = (bf16[64,1024]{1,0:T(8,128)(2,1)S(1)}, bf16[64,1024]{1,0:T(8,128)(2,1)}, u32[]{:S(2)}) copy-start(bf16[64,1024]{1,0:T(8,128)(2,1)} %param.7) | copy-start | bytes 393220

commit v7 on v6

--- a/solution.py
+++ b/solution.py
@@ -8,6 +8,7 @@
 
 LOSS_SCALE = 0.0625
 DECAY = 0.1
+MARK = 64.0
 TB = 128
 SIDE = 4
 BF16 = jnp.bfloat16
@@ -28,26 +29,21 @@
 
 def item_kernel(
     rows_ref, cols_ref, layer_ref, user_ref, user_t_ref, own_ref, other_ref, rating_ref,
-    mask_ref, keep_ref, send_ref, residual_ref, item_acc_ref,
+    keep_ref, send_ref, residual_ref, item_acc_ref,
 ):
     layer = layer_ref[0]
-    tiles, words = mask_ref.shape[:2]
+    tiles = rating_ref.shape[0]
     shards, half_blocks = own_ref.shape[:2]
     per_shard = tiles // shards
 
     item_acc_ref[...] = jnp.zeros_like(item_acc_ref)
 
-    bit = jnp.left_shift(jnp.int32(1), lax.broadcasted_iota(jnp.int32, (8, TB), 0))
     for t in range(tiles):
         b, c = tile_place(rows_ref, cols_ref, t, tiles)
         item = item_block(own_ref, other_ref, layer, t // per_shard, c)
         scores = jnp.dot(user_t_ref[b], item, preferred_element_type=F32)
-        difference = scores - rating_ref[t].astype(F32)
-        parts = []
-        for w in range(words):
-            word = jnp.broadcast_to(mask_ref[t, w:w + 1, :], (8, TB))
-            parts.append(jnp.where((word & bit) != 0, difference[w * 8:(w + 1) * 8], 0.0))
-        residual_ref[t] = jnp.concatenate(parts, axis=0).astype(BF16)
+        rating = rating_ref[t].astype(F32)
+        residual_ref[t] = jnp.where(rating < MARK, scores - rating, 0.0).astype(BF16)
 
     for t in range(tiles):
         b, c = tile_place(rows_ref, cols_ref, t, tiles)
@@ -94,7 +90,7 @@
     return pl.BlockSpec(shape, lambda i, *_: (0,) * len(shape))
 
 
-def item_terms(places, user_factors, user_t, own, other, ratings, masks):
+def item_terms(places, user_factors, user_t, own, other, ratings):
     _, half_blocks, rank, _ = own.shape
     tiles = ratings.shape[0] // SIDE
     return pl.pallas_call(
@@ -103,7 +99,7 @@
             num_scalar_prefetch=3,
             grid=(SIDE,),
             in_specs=[whole(user_factors.shape), whole(user_t.shape)]
-            + [over_shards(x.shape) for x in (own, other, ratings, masks)],
+            + [over_shards(x.shape) for x in (own, other, ratings)],
             out_specs=[over_shards(x.shape) for x in (own, own, ratings)],
             scratch_shapes=[
                 pltpu.VMEM((own.shape[0] // SIDE * 2 * half_blocks, rank, TB), F32),
@@ -112,7 +108,7 @@
         out_shape=[jax.ShapeDtypeStruct(x.shape, BF16) for x in (own, own, ratings)],
         compiler_params=pltpu.CompilerParams(vmem_limit_bytes=16 * 1024 * 1024),
         name="item_terms",
-    )(*places, user_factors, user_t, own, other, ratings, masks)
+    )(*places, user_factors, user_t, own, other, ratings)
 
 
 def user_terms(places, own, other, residual, user_blocks):
@@ -133,24 +129,37 @@
     )(*places, own, other, residual)
 
 
-def ready_kernel(user_ref, masks_ref, user_t_ref, bits_ref):
+def ready_kernel(user_ref, rating_ref, mask_ref, user_t_ref, marked_ref):
     for b in range(user_t_ref.shape[0]):
         block = user_ref[:, b * TB:(b + 1) * TB].astype(F32)
         user_t_ref[b] = block.T.astype(BF16)
-    bits_ref[...] = masks_ref[...]
-
-
-def ready(user_factors, masks):
+    bit = jnp.left_shift(jnp.int32(1), lax.broadcasted_iota(jnp.int32, (8, TB), 0))
+
+    def group(i, carry):
+        for t in range(8):
+            at = i * 8 + t
+            rating = rating_ref[at].astype(F32)
+            parts = []
+            for w in range(mask_ref.shape[1]):
+                word = jnp.broadcast_to(mask_ref[at, w:w + 1, :], (8, TB))
+                parts.append(jnp.where((word & bit) != 0, rating[w * 8:(w + 1) * 8], MARK))
+            marked_ref[at] = jnp.concatenate(parts, axis=0).astype(BF16)
+        return carry
+
+    lax.fori_loop(0, rating_ref.shape[0] // 8, group, 0)
+
+
+def ready(user_factors, ratings, masks):
     rank, users = user_factors.shape
     return pl.pallas_call(
         ready_kernel,
         out_shape=(
             jax.ShapeDtypeStruct((users // TB, TB, rank), BF16),
-            jax.ShapeDtypeStruct(masks.shape, masks.dtype),
-        ),
-        compiler_params=pltpu.CompilerParams(vmem_limit_bytes=8 * 1024 * 1024),
+            jax.ShapeDtypeStruct(ratings.shape, ratings.dtype),
+        ),
+        compiler_params=pltpu.CompilerParams(vmem_limit_bytes=24 * 1024 * 1024),
         name="ready",
-    )(user_factors, masks)
+    )(user_factors, ratings, masks)
 
 
 def spread(block, axes):
@@ -171,12 +180,12 @@
         own = spread(spread(mine.transpose(1, 0, 2), "item_z"), "item_x")
         own = own.reshape(SIDE * SIDE, half_blocks, rank, TB)
         other = lax.ppermute(own, "layer", swap)
-        user_t, bits = ready(user_factors, masks)
-        other, user_t, bits = lax.optimization_barrier((other, user_t, bits))
+        user_t, marked = ready(user_factors, ratings, masks)
+        other, user_t, marked = lax.optimization_barrier((other, user_t, marked))
 
     with jax.named_scope("tiles"):
         places = (tile_rows, tile_cols, layer.reshape(1).astype(jnp.int32))
-        keep, send, residual = item_terms(places, user_factors, user_t, own, other, ratings, bits)
+        keep, send, residual = item_terms(places, user_factors, user_t, own, other, marked)
         user_part = user_terms(places, own, other, residual, user_factors.shape[1] // TB)
 
     with jax.named_scope("scatter_items"):

time: 115 us -> 114 us (level)
  waiting for transfers between devices: 2.14 us -> 0.01 us
  local copies, waits for them, and re-layouts: 1.6 us -> 2.85 us
    ppermute x1, waiting for transfers between devices: 2.13 us -> 0.01 us  [body(): other = lax.ppermute(own, 'layer', swap)]
    pallas_call x1, Pallas kernels: 0.11 us -> 1.38 us  [ready(): pl.pallas_call(ready_kernel, out_shape=(jax.ShapeDtypeStruct((users // TB...]
    unnamed x13, local copies, waits for them, and re-layouts: 0.96 us -> 2.2 us
  transfers between devices with their start and end apart: 2 -> 2, of which waited for: 1 -> 0; matrix products, arithmetic and copies ran while one was open for 0% -> 0% of each run, Pallas kernels for 2% -> 4%
where the time goes in v7:
time: 114 us
  blocking collectives  92 us (81%)
  Pallas kernels  8.26 us (7%)
  starting transfers between devices  7.97 us (7%)
  local copies, waits for them, and re-layouts  2.85 us (2%)
  other arithmetic  2.16 us (2%)
    all_to_all x3, blocking collectives, spread(): return lax.all_to_all(copies, axes, 0, 0)  36.4 us
    all_to_all x1, blocking collectives, body(): part = lax.all_to_all(copies, ('user_z', 'item_z'), 0, 0).astype(F32).sum(0)  24.8 us
    all_to_all x1, blocking collectives, body(): part = lax.all_to_all(both, ('item_x', 'user_y'), 0, 0)  20.7 us
    all_gather x1, blocking collectives, body(): lax.all_gather(jnp.concatenate([item_half, user_part], axis=0), 'layer')  10.1 us
    ppermute x1, starting transfers between devices, body(): other = lax.ppermute(own, 'layer', swap)  6.04 us
    pallas_call x1, Pallas kernels, item_terms(): pl.pallas_call(item_kernel, grid_spec=pltpu.PrefetchScalarGridSpec(num_sc...  4.21 us
    pallas_call x1, Pallas kernels, user_terms(): pl.pallas_call(user_kernel, grid_spec=pltpu.PrefetchScalarGridSpec(num_sc...  2.67 us
  transfers between devices with their start and end apart: 2, of which 0 were waited for; matrix products, arithmetic and copies ran while one was open for 0% of the time, Pallas kernels for 4%

profile of v7, /device:TPU:1, one launch (start us, length us, event | category | flops | bytes accessed | tf_op | source)
XLA Modules:
  0.0 114.1 jit_solution(12737161798632334865)
XLA Ops:
  0.6 0.0 copy-start.2
  0.6 1.0 copy.24
  1.6 0.0 copy-start
  1.7 12.5 %all_to_all.25 = bf16[4,4,64,128]{3,2,1,0:T(8,128)(2,1)S(1)} all-to-all(bf16[4,4,64,128]{3,2,1,0:T(8,128)(2,1)S(1)} %broadcast_in_dim.8), channel_id=1, replica_groups=mesh['user_y'=4,'user_z'=4,'item_x'=4,'item_z'=4,'layer'=2] {'item_z'}, dimensions={0} | all-to-all | bytes 524288 | tf_op jit(solution)/shard_map/gather_items/all_to_all | solution.py:167
  14.2 0.0 copy-start.3
  14.2 0.0 copy-start.4
  14.2 0.2 broadcast_in_dim.9
  14.5 16.6 %all_to_all.26 = bf16[4,4,4,64,128]{4,3,2,1,0:T(8,128)(2,1)S(1)} all-to-all(bf16[4,4,4,64,128]{4,3,2,1,0:T(8,128)(2,1)S(1)} %broadcast_in_dim.9), channel_id=1, replica_groups=mesh['user_y'=4,'user_z'=4,'item_x'=4,'item_z'=4,'layer'=2] {'item_x'}, dimensions={0} | all-to-all | bytes 2097152 | tf_op jit(solution)/shard_map/gather_items/all_to_all | solution.py:167
  31.1 6.0 %collective-permute-start = (bf16[16,4,64,128]{3,2,1,0:T(8,128)(2,1)S(1)}, bf16[16,4,64,128]{3,2,1,0:T(8,128)(2,1)S(1)}, u32[]{:S(2)}, u32[]{:S(2)}) collective-permute-start(bf16[16,4,64,128]{3,2,1,0:T(8,128)(2,1)S(1)} %bitcast.25), channel_id=1, source_target_pairs={{0,1},{1,0},{2,3},{3,2},{4,5},{5,4},{6,7},{7,6},{8,9},{9,8},{10,11... | collective-permute-start | bytes 3145736 | tf_op jit(solution)/shard_map/gather_items/ppermute | solution.py:182
  37.2 0.0 copy-done.2
  37.2 0.0 copy-done
  37.2 0.0 copy-start.1
  37.2 1.2 %copy-done.1 = s32[128,16,128]{2,1,0:T(8,128)S(1)} copy-done((s32[128,16,128]{2,1,0:T(8,128)S(1)}, s32[128,16,128]{2,1,0:T(8,128)}, u32[]{:S(2)}) %copy-start.1) | copy-done | bytes 1048600
  38.4 1.4 %ready.1 = (bf16[4,128,64]{2,1,0:T(8,128)(2,1)S(1)}, bf16[128,128,128]{2,1,0:T(8,128)(2,1)S(1)}) custom-call(bf16[64,512]{1,0:T(8,128)(2,1)S(1)} %copy-done.2, bf16[128,128,128]{2,1,0:T(8,128)(2,1)S(1)} %copy-done, s32[128,16,128]{2,1,0:T(8,128)S(1)} %copy-done.1), custom_call_target="tpu_custom_call" | custom-call | tf_op jit(solution)/shard_map/gather_items/ready/pallas_call | solution.py:154
  39.8 0.0 collective-permute-done.other_ref
  39.8 0.0 copy-done.3
  39.8 0.0 copy-done.4
  39.8 4.2 %item_terms.1 = (bf16[16,4,64,128]{3,2,1,0:T(8,128)(2,1)S(1)}, bf16[16,4,64,128]{3,2,1,0:T(8,128)(2,1)S(1)}, bf16[128,128,128]{2,1,0:T(8,128)(2,1)S(1)}) custom-call(s32[128]{0:T(128)S(1)} %copy-done.3, s32[128]{0:T(128)S(1)} %copy-done.4, s32[1]{0:T(128)} %bitcast.layer_ref, bf16[64,512]{1,0:T(8,128)(2,1)S(1)} %copy-done.2, ...), custom_call_target="tpu_custom_call" | custom-call | tf_op jit(solution)/shard_map/tiles/item_terms/pallas_call | solution.py:96
  44.0 1.9 %collective-permute-start.1 = (bf16[16,4,64,128]{3,2,1,0:T(8,128)(2,1)S(1)}, bf16[16,4,64,128]{3,2,1,0:T(8,128)(2,1)S(1)}, u32[]{:S(2)}, u32[]{:S(2)}) collective-permute-start(bf16[16,4,64,128]{3,2,1,0:T(8,128)(2,1)S(1)} %get-tuple-element.18), channel_id=1, source_target_pairs={{0,1},{1,0},{2,3},{3,2},{4,5},{5,4},{6,7},{7,6},{8,9},{9,8},{10,11... | collective-permute-start | bytes 3145736 | tf_op jit(solution)/shard_map/scatter_items/ppermute | solution.py:192
  46.0 2.7 %user_terms.1 = f32[4,64,128]{2,1,0:T(8,128)S(1)} custom-call(s32[128]{0:T(128)S(1)} %copy-done.3, s32[128]{0:T(128)S(1)} %copy-done.4, s32[1]{0:T(128)} %bitcast.layer_ref, bf16[16,4,64,128]{3,2,1,0:T(8,128)(2,1)S(1)} %bitcast.27, bf16[16,4,64,128]{3,2,1,0:T(8,128)(2,1)S(1)} %collective-permute-done.other_ref, ...), custom_call_target="tpu_custom_call" | custom-call | tf_op jit(solution)/shard_map/tiles/user_terms/pallas_call | solution.py:117
  48.6 0.0 collective-permute-done.1
  48.7 0.4 add_convert_fusion
  49.1 0.1 copy.20
  49.2 0.0 copy-start.5
  49.2 20.7 %all_to_all.27 = bf16[16,4,64,128]{3,2,1,0:T(8,128)(2,1)S(1)} all-to-all(bf16[16,4,64,128]{3,2,1,0:T(8,128)(2,1)S(1)} %bitcast.29), channel_id=1, replica_groups=mesh['user_y'=4,'user_z'=4,'item_x'=4,'item_z'=4,'layer'=2] {'item_x','u..., dimensions={0} | all-to-all | bytes 2097152 | tf_op jit(solution)/shard_map/scatter_items/all_to_all | solution.py:197
  69.9 0.2 reduce_sum.21
  70.2 24.8 %all_to_all.28 = bf16[16,64,128]{2,1,0:T(8,128)(2,1)S(1)} all-to-all(bf16[16,64,128]{2,1,0:T(8,128)(2,1)S(1)} %bitcast.32), channel_id=1, replica_groups=mesh['user_y'=4,'user_z'=4,'item_x'=4,'item_z'=4,'layer'=2] {'user_z','i..., dimensions={0} | all-to-all | bytes 524288 | tf_op jit(solution)/shard_map/sum_along_z/all_to_all | solution.py:203
  95.0 7.2 %all_to_all.29 = f32[4,64,128]{2,1,0:T(8,128)S(1)} all-to-all(f32[4,64,128]{2,1,0:T(8,128)S(1)} %broadcast_in_dim.11), channel_id=1, replica_groups=mesh['user_y'=4,'user_z'=4,'item_x'=4,'item_z'=4,'layer'=2] {'user_y'}, dimensions={0} | all-to-all | bytes 262144 | tf_op jit(solution)/shard_map/join/all_to_all | solution.py:167
  102.3 10.1 %all-gather = f32[16,64,128]{2,1,0:T(8,128)S(1)} all-gather(f32[8,64,128]{2,1,0:T(8,128)S(1)} %pad_maximum_fusion), channel_id=2, replica_groups=mesh['user_y'=4,'user_z'=4,'item_x'=4,'item_z'=4,'layer'=2] {'layer'}, dimensions={0}, use_global_device_ids=true | all-gather | bytes 786432 | tf_op jit(solution)/shard_map/join/all_gather | solution.py:207
  112.4 0.7 bitcast_add_fusion.1
  113.1 0.2 copy.22
  113.3 0.0 copy-done.5
  113.3 0.8 bitcast_add_fusion
  (8 shorter events, 0.2 us)
Async XLA Ops:
  0.6 36.5 %copy-start.2 = (bf16[64,512]{1,0:T(8,128)(2,1)S(1)}, bf16[64,512]{1,0:T(8,128)(2,1)}, u32[]{:S(2)}) copy-start(bf16[64,512]{1,0:T(8,128)(2,1)} %user_ref.3) | copy-start | bytes 196612
  1.6 35.6 %copy-start = (bf16[128,128,128]{2,1,0:T(8,128)(2,1)S(1)}, bf16[128,128,128]{2,1,0:T(8,128)(2,1)}, u32[]{:S(2)}) copy-start(bf16[128,128,128]{2,1,0:T(8,128)(2,1)} %rating_ref.1) | copy-start | bytes 12582916
  14.2 25.6 %copy-start.3 = (s32[128]{0:T(128)S(1)}, s32[128]{0:T(128)}, u32[]{:S(2)}) copy-start(s32[128]{0:T(128)} %rows_ref.3) | copy-start | bytes 1540
  14.2 25.6 %copy-start.4 = (s32[128]{0:T(128)S(1)}, s32[128]{0:T(128)}, u32[]{:S(2)}) copy-start(s32[128]{0:T(128)} %cols_ref.3) | copy-start | bytes 1540
  31.1 8.7 %collective-permute-start = (bf16[16,4,64,128]{3,2,1,0:T(8,128)(2,1)S(1)}, bf16[16,4,64,128]{3,2,1,0:T(8,128)(2,1)S(1)}, u32[]{:S(2)}, u32[]{:S(2)}) collective-permute-start(bf16[16,4,64,128]{3,2,1,0:T(8,128)(2,1)S(1)} %bitcast.25), channel_id=1, source_target_pairs={{0,1},{1,0},{2,3},{3,2},{4,5},{5,4},{6,7},{7,6},{8,9},{9,8},{10,11... | collective-permute-start | bytes 3145736 | tf_op jit(solution)/shard_map/gather_items/ppermute | solution.py:182
  37.2 1.2 %copy-start.1 = (s32[128,16,128]{2,1,0:T(8,128)S(1)}, s32[128,16,128]{2,1,0:T(8,128)}, u32[]{:S(2)}) copy-start(s32[128,16,128]{2,1,0:T(8,128)} %mask_ref.1) | copy-start | bytes 3145732
  44.0 4.6 %collective-permute-start.1 = (bf16[16,4,64,128]{3,2,1,0:T(8,128)(2,1)S(1)}, bf16[16,4,64,128]{3,2,1,0:T(8,128)(2,1)S(1)}, u32[]{:S(2)}, u32[]{:S(2)}) collective-permute-start(bf16[16,4,64,128]{3,2,1,0:T(8,128)(2,1)S(1)} %get-tuple-element.18), channel_id=1, source_target_pairs={{0,1},{1,0},{2,3},{3,2},{4,5},{5,4},{6,7},{7,6},{8,9},{9,8},{10,11... | collective-permute-start | bytes 3145736 | tf_op jit(solution)/shard_map/scatter_items/ppermute | solution.py:192
  49.2 64.1 %copy-start.5 = (bf16[64,1024]{1,0:T(8,128)(2,1)S(1)}, bf16[64,1024]{1,0:T(8,128)(2,1)}, u32[]{:S(2)}) copy-start(bf16[64,1024]{1,0:T(8,128)(2,1)} %param.7) | copy-start | bytes 393220

commit v8 on v7

--- a/solution.py
+++ b/solution.py
@@ -203,13 +203,12 @@
         part = lax.all_to_all(copies, ("user_z", "item_z"), 0, 0).astype(F32).sum(0)
 
     with jax.named_scope("join"):
-        item_half = spread(part, "user_y")
-        joined = lax.all_gather(jnp.concatenate([item_half, user_part], axis=0), "layer")
-        item_total = joined[:, :half_blocks].reshape(2 * half_blocks, rank, TB)
-        user_total = joined[0, half_blocks:] + joined[1, half_blocks:]
-        item_total = item_total.transpose(1, 0, 2).reshape(rank, shard_len)
+        joined = lax.all_gather(jnp.concatenate([part[None], user_part], axis=0), "layer")
+        user_total = joined[0, 1:] + joined[1, 1:]
         user_total = user_total.transpose(1, 0, 2).reshape(user_factors.shape)
         grad_users = LOSS_SCALE * user_total + DECAY * user_factors.astype(F32)
+        pieces, grad_users = lax.optimization_barrier((joined[:, 0], grad_users))
+        item_total = spread(pieces, "user_y").transpose(2, 1, 0, 3).reshape(rank, shard_len)
         grad_items = LOSS_SCALE * item_total + DECAY * item_factors.astype(F32)
     return (grad_users, grad_items)
 

time: 114 us -> 115 us (level); the launches traced: 114 us -> 114 us
    all_gather x1, blocking collectives: 10.1 us -> 8.61 us  [body(): lax.all_gather(jnp.concatenate([part[None], user_part], axis=0), 'layer')]
where the time goes in v8:
time: 115 us; the launch traced here: 114 us
  blocking collectives  91.5 us (80%)
  Pallas kernels  8.26 us (7%)
  starting transfers between devices  7.98 us (7%)
  local copies, waits for them, and re-layouts  3.08 us (3%)
  other arithmetic  2.24 us (2%)
    all_to_all x3, blocking collectives, spread(): return lax.all_to_all(copies, axes, 0, 0)  37.3 us
    all_to_all x1, blocking collectives, body(): part = lax.all_to_all(copies, ('user_z', 'item_z'), 0, 0).astype(F32).sum(0)  24.8 us
    all_to_all x1, blocking collectives, body(): part = lax.all_to_all(both, ('item_x', 'user_y'), 0, 0)  20.7 us
    all_gather x1, blocking collectives, body(): lax.all_gather(jnp.concatenate([part[None], user_part], axis=0), 'layer')  8.61 us
    ppermute x1, starting transfers between devices, body(): other = lax.ppermute(own, 'layer', swap)  6.04 us
    pallas_call x1, Pallas kernels, item_terms(): pl.pallas_call(item_kernel, grid_spec=pltpu.PrefetchScalarGridSpec(num_sc...  4.2 us
    pallas_call x1, Pallas kernels, user_terms(): pl.pallas_call(user_kernel, grid_spec=pltpu.PrefetchScalarGridSpec(num_sc...  2.68 us
  transfers between devices with their start and end apart: 2, of which 0 were waited for; matrix products, arithmetic and copies ran while one was open for 0% of the time, Pallas kernels for 4%

profile of v8, /device:TPU:1, one launch (start us, length us, event | category | flops | bytes accessed | tf_op | source)
XLA Modules:
  0.0 113.9 jit_solution(2571532795509832958)
XLA Ops:
  0.6 0.0 copy-start.2
  0.6 1.0 copy.30
  1.6 0.0 copy-start
  1.7 12.5 %all_to_all.25 = bf16[4,4,64,128]{3,2,1,0:T(8,128)(2,1)S(1)} all-to-all(bf16[4,4,64,128]{3,2,1,0:T(8,128)(2,1)S(1)} %broadcast_in_dim.10), channel_id=1, replica_groups=mesh['user_y'=4,'user_z'=4,'item_x'=4,'item_z'=4,'layer'=2] {'item_z'}, dimensions={0} | all-to-all | bytes 524288 | tf_op jit(solution)/shard_map/gather_items/all_to_all | solution.py:167
  14.2 0.0 copy-start.3
  14.2 0.0 copy-start.4
  14.2 0.2 broadcast_in_dim.11
  14.5 16.6 %all_to_all.26 = bf16[4,4,4,64,128]{4,3,2,1,0:T(8,128)(2,1)S(1)} all-to-all(bf16[4,4,4,64,128]{4,3,2,1,0:T(8,128)(2,1)S(1)} %broadcast_in_dim.11), channel_id=1, replica_groups=mesh['user_y'=4,'user_z'=4,'item_x'=4,'item_z'=4,'layer'=2] {'item_x'}, dimensions={0} | all-to-all | bytes 2097152 | tf_op jit(solution)/shard_map/gather_items/all_to_all | solution.py:167
  31.1 6.0 %collective-permute-start = (bf16[16,4,64,128]{3,2,1,0:T(8,128)(2,1)S(1)}, bf16[16,4,64,128]{3,2,1,0:T(8,128)(2,1)S(1)}, u32[]{:S(2)}, u32[]{:S(2)}) collective-permute-start(bf16[16,4,64,128]{3,2,1,0:T(8,128)(2,1)S(1)} %bitcast.25), channel_id=1, source_target_pairs={{0,1},{1,0},{2,3},{3,2},{4,5},{5,4},{6,7},{7,6},{8,9},{9,8},{10,11... | collective-permute-start | bytes 3145736 | tf_op jit(solution)/shard_map/gather_items/ppermute | solution.py:182
  37.2 0.0 copy-done.2
  37.2 0.0 copy-done
  37.2 0.0 copy-start.1
  37.2 1.2 %copy-done.1 = s32[128,16,128]{2,1,0:T(8,128)S(1)} copy-done((s32[128,16,128]{2,1,0:T(8,128)S(1)}, s32[128,16,128]{2,1,0:T(8,128)}, u32[]{:S(2)}) %copy-start.1) | copy-done | bytes 1048600
  38.4 1.4 %ready.1 = (bf16[4,128,64]{2,1,0:T(8,128)(2,1)S(1)}, bf16[128,128,128]{2,1,0:T(8,128)(2,1)S(1)}) custom-call(bf16[64,512]{1,0:T(8,128)(2,1)S(1)} %copy-done.2, bf16[128,128,128]{2,1,0:T(8,128)(2,1)S(1)} %copy-done, s32[128,16,128]{2,1,0:T(8,128)S(1)} %copy-done.1), custom_call_target="tpu_custom_call" | custom-call | tf_op jit(solution)/shard_map/gather_items/ready/pallas_call | solution.py:154
  39.8 0.0 collective-permute-done.other_ref
  39.8 0.0 copy-done.3
  39.8 0.0 copy-done.4
  39.8 4.2 %item_terms.1 = (bf16[16,4,64,128]{3,2,1,0:T(8,128)(2,1)S(1)}, bf16[16,4,64,128]{3,2,1,0:T(8,128)(2,1)S(1)}, bf16[128,128,128]{2,1,0:T(8,128)(2,1)S(1)}) custom-call(s32[128]{0:T(128)S(1)} %copy-done.3, s32[128]{0:T(128)S(1)} %copy-done.4, s32[1]{0:T(128)} %bitcast.layer_ref, bf16[64,512]{1,0:T(8,128)(2,1)S(1)} %copy-done.2, ...), custom_call_target="tpu_custom_call" | custom-call | tf_op jit(solution)/shard_map/tiles/item_terms/pallas_call | solution.py:96
  44.0 1.9 %collective-permute-start.1 = (bf16[16,4,64,128]{3,2,1,0:T(8,128)(2,1)S(1)}, bf16[16,4,64,128]{3,2,1,0:T(8,128)(2,1)S(1)}, u32[]{:S(2)}, u32[]{:S(2)}) collective-permute-start(bf16[16,4,64,128]{3,2,1,0:T(8,128)(2,1)S(1)} %get-tuple-element.20), channel_id=1, source_target_pairs={{0,1},{1,0},{2,3},{3,2},{4,5},{5,4},{6,7},{7,6},{8,9},{9,8},{10,11... | collective-permute-start | bytes 3145736 | tf_op jit(solution)/shard_map/scatter_items/ppermute | solution.py:192
  46.0 2.7 %user_terms.1 = f32[4,64,128]{2,1,0:T(8,128)S(1)} custom-call(s32[128]{0:T(128)S(1)} %copy-done.3, s32[128]{0:T(128)S(1)} %copy-done.4, s32[1]{0:T(128)} %bitcast.layer_ref, bf16[16,4,64,128]{3,2,1,0:T(8,128)(2,1)S(1)} %bitcast.27, bf16[16,4,64,128]{3,2,1,0:T(8,128)(2,1)S(1)} %collective-permute-done.other_ref, ...), custom_call_target="tpu_custom_call" | custom-call | tf_op jit(solution)/shard_map/tiles/user_terms/pallas_call | solution.py:117
  48.7 0.0 collective-permute-done.1
  48.7 0.4 add_convert_fusion
  49.1 0.1 copy.25
  49.2 0.0 copy-start.5
  49.2 20.7 %all_to_all.27 = bf16[16,4,64,128]{3,2,1,0:T(8,128)(2,1)S(1)} all-to-all(bf16[16,4,64,128]{3,2,1,0:T(8,128)(2,1)S(1)} %bitcast.29), channel_id=1, replica_groups=mesh['user_y'=4,'user_z'=4,'item_x'=4,'item_z'=4,'layer'=2] {'item_x','u..., dimensions={0} | all-to-all | bytes 2097152 | tf_op jit(solution)/shard_map/scatter_items/all_to_all | solution.py:197
  69.9 0.2 reduce_sum.21
  70.2 24.8 %all_to_all.28 = bf16[16,64,128]{2,1,0:T(8,128)(2,1)S(1)} all-to-all(bf16[16,64,128]{2,1,0:T(8,128)(2,1)S(1)} %bitcast.32), channel_id=1, replica_groups=mesh['user_y'=4,'user_z'=4,'item_x'=4,'item_z'=4,'layer'=2] {'user_z','i..., dimensions={0} | all-to-all | bytes 524288 | tf_op jit(solution)/shard_map/sum_along_z/all_to_all | solution.py:203
  95.1 8.6 %all-gather = f32[10,64,128]{2,1,0:T(8,128)S(1)} all-gather(f32[5,64,128]{2,1,0:T(8,128)S(1)} %pad_maximum_fusion), channel_id=2, replica_groups=mesh['user_y'=4,'user_z'=4,'item_x'=4,'item_z'=4,'layer'=2] {'layer'}, dimensions={0}, use_global_device_ids=true | all-gather | bytes 491520 | tf_op jit(solution)/shard_map/join/all_gather | solution.py:206
  103.7 0.7 bitcast_add_fusion
  104.4 0.1 copy.27
  104.4 0.1 broadcast_in_dim.14
  104.5 8.2 %all_to_all.29 = f32[4,2,64,128]{3,1,2,0:T(2,128)S(1)} all-to-all(f32[4,2,64,128]{3,1,2,0:T(2,128)S(1)} %broadcast_in_dim.14), channel_id=1, replica_groups=mesh['user_y'=4,'user_z'=4,'item_x'=4,'item_z'=4,'layer'=2] {'user_y'}, dimensions={0} | all-to-all | bytes 524288 | tf_op jit(solution)/shard_map/join/all_to_all | solution.py:167
  112.7 0.1 multiply_bitcast_fusion
  112.9 0.2 copy.28
  113.0 0.1 mul.53
  113.2 0.0 copy-done.5
  113.2 0.7 multiply_add_fusion
  (7 shorter events, 0.2 us)
Async XLA Ops:
  0.6 36.5 %copy-start.2 = (bf16[64,512]{1,0:T(8,128)(2,1)S(1)}, bf16[64,512]{1,0:T(8,128)(2,1)}, u32[]{:S(2)}) copy-start(bf16[64,512]{1,0:T(8,128)(2,1)} %user_ref.3) | copy-start | bytes 196612
  1.6 35.6 %copy-start = (bf16[128,128,128]{2,1,0:T(8,128)(2,1)S(1)}, bf16[128,128,128]{2,1,0:T(8,128)(2,1)}, u32[]{:S(2)}) copy-start(bf16[128,128,128]{2,1,0:T(8,128)(2,1)} %rating_ref.1) | copy-start | bytes 12582916
  14.2 25.6 %copy-start.3 = (s32[128]{0:T(128)S(1)}, s32[128]{0:T(128)}, u32[]{:S(2)}) copy-start(s32[128]{0:T(128)} %rows_ref.3) | copy-start | bytes 1540
  14.2 25.6 %copy-start.4 = (s32[128]{0:T(128)S(1)}, s32[128]{0:T(128)}, u32[]{:S(2)}) copy-start(s32[128]{0:T(128)} %cols_ref.3) | copy-start | bytes 1540
  31.1 8.7 %collective-permute-start = (bf16[16,4,64,128]{3,2,1,0:T(8,128)(2,1)S(1)}, bf16[16,4,64,128]{3,2,1,0:T(8,128)(2,1)S(1)}, u32[]{:S(2)}, u32[]{:S(2)}) collective-permute-start(bf16[16,4,64,128]{3,2,1,0:T(8,128)(2,1)S(1)} %bitcast.25), channel_id=1, source_target_pairs={{0,1},{1,0},{2,3},{3,2},{4,5},{5,4},{6,7},{7,6},{8,9},{9,8},{10,11... | collective-permute-start | bytes 3145736 | tf_op jit(solution)/shard_map/gather_items/ppermute | solution.py:182
  37.2 1.2 %copy-start.1 = (s32[128,16,128]{2,1,0:T(8,128)S(1)}, s32[128,16,128]{2,1,0:T(8,128)}, u32[]{:S(2)}) copy-start(s32[128,16,128]{2,1,0:T(8,128)} %mask_ref.1) | copy-start | bytes 3145732
  44.0 4.6 %collective-permute-start.1 = (bf16[16,4,64,128]{3,2,1,0:T(8,128)(2,1)S(1)}, bf16[16,4,64,128]{3,2,1,0:T(8,128)(2,1)S(1)}, u32[]{:S(2)}, u32[]{:S(2)}) collective-permute-start(bf16[16,4,64,128]{3,2,1,0:T(8,128)(2,1)S(1)} %get-tuple-element.20), channel_id=1, source_target_pairs={{0,1},{1,0},{2,3},{3,2},{4,5},{5,4},{6,7},{7,6},{8,9},{9,8},{10,11... | collective-permute-start | bytes 3145736 | tf_op jit(solution)/shard_map/scatter_items/ppermute | solution.py:192
  49.2 64.0 %copy-start.5 = (bf16[64,1024]{1,0:T(8,128)(2,1)S(1)}, bf16[64,1024]{1,0:T(8,128)(2,1)}, u32[]{:S(2)}) copy-start(bf16[64,1024]{1,0:T(8,128)(2,1)} %param.7) | copy-start | bytes 393220
